TPU v7x, 128 devices: a whole 4x4x4 slice. The times are simulated.
128 devices in a mesh: bx: 16 (over y, x_hi, core), by: 8 (over z, x_lo).
Axes of the slice: x: 4 (x_hi: 2, x_lo: 2; x = x_hi * 2 + x_lo), y: 4, z: 4, core: 2. Of those that a mesh axis runs over, the one named last changes fastest.
Arguments:
- fields: float32 [4, 512, 1024, 128], P(None, 'bx', 'by'), may hold values from -6 to 6
- ground: int32 [512, 1024], P('bx', 'by'), may hold values 0 or 1
- observers: float32 [3, 131072], P(None, 'bx'), may hold values from -1 to 1
- slots: int32 [131072], P('bx'), may hold values from 0 to 62
- fractions: float32 [131072], P('bx'), may hold values from 0 to 1
- owners: int32 [131072, 1], P('bx'), may hold values from 0 to 127; in each aligned block of 8192 rows (0 to 8191, 8192 to 16383, ...) at most 128 rows name the same one
- arrival_cell: int32 [128, 16, 128], P(('bx', 'by')), may hold values from 0 to 524287
- panel_points: float32 [3, 16384], P(None, 'by'), may hold values from -1 to 1
- panel_normals: float32 [3, 16384], P(None, 'by'), may hold values from -4 to 4
- sources: bfloat16 [3, 16384, 64], P(None, 'by'), may hold values from -0.02734375 to 0.02734375
Outputs:
- new_fields: float32 [4, 512, 1024, 128], P(None, 'bx', 'by')
Inputs may be any that keep to these rules, and one draw needn't show every extreme that they name: `owners`: observers are in blocks of 8192 consecutive rows, one block a bx index; within a block no device is named by more than 128 observers, and that most is reached. Device numbers are bx index * 8 + by index. `arrival_cell`: cells are numbered (x * 128 + y) * 128 + z inside a brick; entries past an owner's count for a block are never used.
All inputs are finite; a program needn't handle non-finite values. No bound on the sum of `ground` on one device may be relied on, other than what follows from the above.
Results may differ from a plain program's by a relative error of at most 0.0003.
Values sent between devices are 32-bit elements; how exact they have to be, the bound alone decides.
A program may use at most 128 MiB of HBM per device.

v0:
```python
import jax
import jax.numpy as jnp
from jax import lax
from jax.sharding import PartitionSpec as P

STEPS = 2


STENCIL_WEIGHTS = (0.770882380518, -0.166705904415, 0.02084314277)
TIME_STEP = 0.5
SOFTENING = 0.01


def padded(block, sides, width):
    for axis, dim in sides:
        count = lax.axis_size(axis)
        forward = [(i, i + 1) for i in range(count - 1)]
        backward = [(target, source) for source, target in forward]
        low = lax.ppermute(
            lax.slice_in_dim(block, block.shape[dim] - width, None, axis=dim), axis, forward
        )
        high = lax.ppermute(lax.slice_in_dim(block, 0, width, axis=dim), axis, backward)
        block = jnp.concatenate([low, block, high], axis=dim)
    return block


def centered(grid_field, axis):
    inner_size = grid_field.shape[axis] - 6
    summed = jnp.zeros_like(lax.slice_in_dim(grid_field, 3, 3 + inner_size, axis=axis))
    for offset, weight in enumerate(STENCIL_WEIGHTS, 1):
        forward = lax.slice_in_dim(grid_field, 3 + offset, 3 + offset + inner_size, axis=axis)
        behind = lax.slice_in_dim(grid_field, 3 - offset, 3 - offset + inner_size, axis=axis)
        summed = summed + weight * (forward - behind)
    return summed


def ground_pad(grid_field, ground_flags, parity):
    mirror_cells = parity * ground_flags[:, :, None] * grid_field[:, :, 2::-1]
    top_cells = jnp.zeros(grid_field.shape[:2] + (3,), jnp.float32)
    return jnp.concatenate([mirror_cells, grid_field, top_cells], axis=2)


def velocity_update(pressure_wide, velocity, ground_flags):
    pressure_core = pressure_wide[3:-3, 3:-3]
    grad_x = centered(pressure_wide[:, 3:-3], 0)
    grad_y = centered(pressure_wide[3:-3, :], 1)
    grad_z = centered(ground_pad(pressure_core, ground_flags, 1.0), 2)
    return velocity - TIME_STEP * jnp.stack([grad_x, grad_y, grad_z])


def pressure_update(velocity_wide, pressure, ground_flags):
    div_x = centered(velocity_wide[0][:, 3:-3], 0)
    div_y = centered(velocity_wide[1][3:-3, :], 1)
    div_z = centered(ground_pad(velocity_wide[2][3:-3, 3:-3], ground_flags, -1.0), 2)
    return pressure - TIME_STEP * (div_x + div_y + div_z)


def pressure_rim(pressure):
    return padded(pressure, (("bx", 0), ("by", 1)), 3)


def panel_kernel(points, panel_points, panel_normals):
    offset = points[:, :, None] - panel_points[:, None, :]
    distance_sq = jnp.sum(offset * offset, axis=0) + SOFTENING
    inverse = 1.0 / jnp.sqrt(distance_sq)
    normal_part = jnp.sum(offset * panel_normals[:, None, :], axis=0)
    near_field = normal_part * inverse * inverse
    return jnp.concatenate([inverse, near_field, near_field * inverse], axis=1).astype(jnp.bfloat16)


def observed_values(points, slot_rows, fraction_rows, panel_points, panel_normals, source_matrix):
    kernel = panel_kernel(points, panel_points, panel_normals)
    history = jnp.dot(kernel, source_matrix, preferred_element_type=jnp.float32)
    sample_ids = jnp.arange(history.shape[1], dtype=jnp.int32)[None, :]
    weights = jnp.where(sample_ids == slot_rows[:, None], 1.0 - fraction_rows[:, None], 0.0)
    weights = weights + jnp.where(sample_ids == slot_rows[:, None] + 1, fraction_rows[:, None], 0.0)
    return jnp.sum(history * weights, axis=1)


def body(
    fields,
    ground,
    observers,
    slots,
    fractions,
    owners,
    arrival_cell,
    panel_points,
    panel_normals,
    sources,
):
    rows_here = observers.shape[1]
    block_rows = min(512, rows_here)
    source_matrix = sources.reshape(-1, sources.shape[2])

    def one_block(block_id):
        row_start = block_id * block_rows
        points = lax.dynamic_slice_in_dim(observers, row_start, block_rows, 1)
        slot_rows = lax.dynamic_slice_in_dim(slots, row_start, block_rows, 0)
        fraction_rows = lax.dynamic_slice_in_dim(fractions, row_start, block_rows, 0)
        return observed_values(
            points, slot_rows, fraction_rows, panel_points, panel_normals, source_matrix
        )

    partial_values = lax.map(
        one_block, jnp.arange(rows_here // block_rows, dtype=jnp.int32)
    ).reshape(-1)
    count_bx = lax.axis_size("bx")
    count_by = lax.axis_size("by")
    devices = count_bx * count_by
    capacity = arrival_cell.shape[2]
    target = owners[:, 0]
    onehot = (target[:, None] == jnp.arange(devices, dtype=jnp.int32)[None, :]).astype(jnp.int32)
    slot_rank = jnp.sum(jnp.cumsum(onehot, axis=0) * onehot, axis=1) - 1
    packet = jnp.zeros((devices, capacity), jnp.float32).at[target, slot_rank].set(partial_values)
    arrived = lax.all_to_all(packet, ("bx", "by"), split_axis=0, concat_axis=0, tiled=True)
    received = jnp.sum(arrived.reshape(count_bx, count_by, capacity), axis=1)
    size_x, size_y, size_z = fields.shape[1:]
    pressure = fields[0].reshape(-1).at[arrival_cell[0].reshape(-1)].add(received.reshape(-1))
    pressure = pressure.reshape(size_x, size_y, size_z)
    velocity = fields[1:]
    ground_flags = ground.astype(jnp.float32)
    for _ in range(STEPS):
        velocity = velocity_update(pressure_rim(pressure), velocity, ground_flags)
        velocity_wide = padded(velocity, (("bx", 1), ("by", 2)), 3)
        pressure = pressure_update(velocity_wide, pressure, ground_flags)
    return jnp.concatenate([pressure[None], velocity], axis=0)


def solution(mesh):
    placed = (
        P(None, "bx", "by", None),
        P("bx", "by"),
        P(None, "bx"),
        P("bx"),
        P("bx"),
        P("bx", None),
        P(("bx", "by"), None, None),
        P(None, "by"),
        P(None, "by"),
        P(None, "by", None),
    )
    return jax.shard_map(
        body, mesh=mesh, in_specs=placed, out_specs=P(None, "bx", "by", None), check_vma=False
    )
```

profile of v0, /device:TPU:36, one launch (start us, length us, event | category | flops | bytes accessed | tf_op | source)
XLA Modules:
  0.0 566.4 jit_solution(15352815114331051383)
XLA Ops:
  13.5 237.7 %while.10 = (s32[]{:T(128)}, f32[16,512]{1,0:T(8,128)S(1)}, s32[16]{0:T(128)S(1)}, f32[3,8192]{1,0:T(4,128)}, f32[3,2048]{1,0:T(4,128)S(1)}, /*index=5*/f32[3,20...) while((s32[]{:T(128)}, f32[16,512]{1,0:T(8,128)S(1)}, ...), condition=%wide.region_7.8_spmd, body=%wide.region_3.7_spmd.sunk | while | flops 442728960 | bytes 30240968 | solution.py:105
  15.4 7.5 %fusion.146 = (f32[512,2048]{1,0:T(8,128)S(1)}, f32[512,2048]{1,0:T(8,128)S(1)}) fusion(f32[3,2048]{1,0:T(4,128)S(1)} %get-tuple-element.211, f32[3,512]{1,0:T(4,128)S(1)} %constant_dynamic-slice_fusion.2, f32[3,2048]{1,0:T(4,128)S(1)} %get-tuple-element.212), kind=kLoop, calls=%fused_computation.4.clone.1 | loop fusion | flops 13631488 | bytes 8443904 | tf_op jit(solution)/shard_map/while/body/eval_jaxpr/reduce_sum | solution.py:64
  30.3 7.5 %fusion.146 = (f32[512,2048]{1,0:T(8,128)S(1)}, f32[512,2048]{1,0:T(8,128)S(1)}) fusion(f32[3,2048]{1,0:T(4,128)S(1)} %get-tuple-element.211, f32[3,512]{1,0:T(4,128)S(1)} %constant_dynamic-slice_fusion.2, f32[3,2048]{1,0:T(4,128)S(1)} %get-tuple-element.212), kind=kLoop, calls=%fused_computation.4.clone.1 | loop fusion | flops 13631488 | bytes 8443904 | tf_op jit(solution)/shard_map/while/body/eval_jaxpr/reduce_sum | solution.py:64
  45.1 7.5 %fusion.146 = (f32[512,2048]{1,0:T(8,128)S(1)}, f32[512,2048]{1,0:T(8,128)S(1)}) fusion(f32[3,2048]{1,0:T(4,128)S(1)} %get-tuple-element.211, f32[3,512]{1,0:T(4,128)S(1)} %constant_dynamic-slice_fusion.2, f32[3,2048]{1,0:T(4,128)S(1)} %get-tuple-element.212), kind=kLoop, calls=%fused_computation.4.clone.1 | loop fusion | flops 13631488 | bytes 8443904 | tf_op jit(solution)/shard_map/while/body/eval_jaxpr/reduce_sum | solution.py:64
  60.0 7.5 %fusion.146 = (f32[512,2048]{1,0:T(8,128)S(1)}, f32[512,2048]{1,0:T(8,128)S(1)}) fusion(f32[3,2048]{1,0:T(4,128)S(1)} %get-tuple-element.211, f32[3,512]{1,0:T(4,128)S(1)} %constant_dynamic-slice_fusion.2, f32[3,2048]{1,0:T(4,128)S(1)} %get-tuple-element.212), kind=kLoop, calls=%fused_computation.4.clone.1 | loop fusion | flops 13631488 | bytes 8443904 | tf_op jit(solution)/shard_map/while/body/eval_jaxpr/reduce_sum | solution.py:64
  74.9 7.5 %fusion.146 = (f32[512,2048]{1,0:T(8,128)S(1)}, f32[512,2048]{1,0:T(8,128)S(1)}) fusion(f32[3,2048]{1,0:T(4,128)S(1)} %get-tuple-element.211, f32[3,512]{1,0:T(4,128)S(1)} %constant_dynamic-slice_fusion.2, f32[3,2048]{1,0:T(4,128)S(1)} %get-tuple-element.212), kind=kLoop, calls=%fused_computation.4.clone.1 | loop fusion | flops 13631488 | bytes 8443904 | tf_op jit(solution)/shard_map/while/body/eval_jaxpr/reduce_sum | solution.py:64
  89.7 7.5 %fusion.146 = (f32[512,2048]{1,0:T(8,128)S(1)}, f32[512,2048]{1,0:T(8,128)S(1)}) fusion(f32[3,2048]{1,0:T(4,128)S(1)} %get-tuple-element.211, f32[3,512]{1,0:T(4,128)S(1)} %constant_dynamic-slice_fusion.2, f32[3,2048]{1,0:T(4,128)S(1)} %get-tuple-element.212), kind=kLoop, calls=%fused_computation.4.clone.1 | loop fusion | flops 13631488 | bytes 8443904 | tf_op jit(solution)/shard_map/while/body/eval_jaxpr/reduce_sum | solution.py:64
  104.6 7.5 %fusion.146 = (f32[512,2048]{1,0:T(8,128)S(1)}, f32[512,2048]{1,0:T(8,128)S(1)}) fusion(f32[3,2048]{1,0:T(4,128)S(1)} %get-tuple-element.211, f32[3,512]{1,0:T(4,128)S(1)} %constant_dynamic-slice_fusion.2, f32[3,2048]{1,0:T(4,128)S(1)} %get-tuple-element.212), kind=kLoop, calls=%fused_computation.4.clone.1 | loop fusion | flops 13631488 | bytes 8443904 | tf_op jit(solution)/shard_map/while/body/eval_jaxpr/reduce_sum | solution.py:64
  119.4 7.5 %fusion.146 = (f32[512,2048]{1,0:T(8,128)S(1)}, f32[512,2048]{1,0:T(8,128)S(1)}) fusion(f32[3,2048]{1,0:T(4,128)S(1)} %get-tuple-element.211, f32[3,512]{1,0:T(4,128)S(1)} %constant_dynamic-slice_fusion.2, f32[3,2048]{1,0:T(4,128)S(1)} %get-tuple-element.212), kind=kLoop, calls=%fused_computation.4.clone.1 | loop fusion | flops 13631488 | bytes 8443904 | tf_op jit(solution)/shard_map/while/body/eval_jaxpr/reduce_sum | solution.py:64
  134.3 7.5 %fusion.146 = (f32[512,2048]{1,0:T(8,128)S(1)}, f32[512,2048]{1,0:T(8,128)S(1)}) fusion(f32[3,2048]{1,0:T(4,128)S(1)} %get-tuple-element.211, f32[3,512]{1,0:T(4,128)S(1)} %constant_dynamic-slice_fusion.2, f32[3,2048]{1,0:T(4,128)S(1)} %get-tuple-element.212), kind=kLoop, calls=%fused_computation.4.clone.1 | loop fusion | flops 13631488 | bytes 8443904 | tf_op jit(solution)/shard_map/while/body/eval_jaxpr/reduce_sum | solution.py:64
  149.1 7.5 %fusion.146 = (f32[512,2048]{1,0:T(8,128)S(1)}, f32[512,2048]{1,0:T(8,128)S(1)}) fusion(f32[3,2048]{1,0:T(4,128)S(1)} %get-tuple-element.211, f32[3,512]{1,0:T(4,128)S(1)} %constant_dynamic-slice_fusion.2, f32[3,2048]{1,0:T(4,128)S(1)} %get-tuple-element.212), kind=kLoop, calls=%fused_computation.4.clone.1 | loop fusion | flops 13631488 | bytes 8443904 | tf_op jit(solution)/shard_map/while/body/eval_jaxpr/reduce_sum | solution.py:64
  164.0 7.5 %fusion.146 = (f32[512,2048]{1,0:T(8,128)S(1)}, f32[512,2048]{1,0:T(8,128)S(1)}) fusion(f32[3,2048]{1,0:T(4,128)S(1)} %get-tuple-element.211, f32[3,512]{1,0:T(4,128)S(1)} %constant_dynamic-slice_fusion.2, f32[3,2048]{1,0:T(4,128)S(1)} %get-tuple-element.212), kind=kLoop, calls=%fused_computation.4.clone.1 | loop fusion | flops 13631488 | bytes 8443904 | tf_op jit(solution)/shard_map/while/body/eval_jaxpr/reduce_sum | solution.py:64
  178.9 7.5 %fusion.146 = (f32[512,2048]{1,0:T(8,128)S(1)}, f32[512,2048]{1,0:T(8,128)S(1)}) fusion(f32[3,2048]{1,0:T(4,128)S(1)} %get-tuple-element.211, f32[3,512]{1,0:T(4,128)S(1)} %constant_dynamic-slice_fusion.2, f32[3,2048]{1,0:T(4,128)S(1)} %get-tuple-element.212), kind=kLoop, calls=%fused_computation.4.clone.1 | loop fusion | flops 13631488 | bytes 8443904 | tf_op jit(solution)/shard_map/while/body/eval_jaxpr/reduce_sum | solution.py:64
  193.7 7.5 %fusion.146 = (f32[512,2048]{1,0:T(8,128)S(1)}, f32[512,2048]{1,0:T(8,128)S(1)}) fusion(f32[3,2048]{1,0:T(4,128)S(1)} %get-tuple-element.211, f32[3,512]{1,0:T(4,128)S(1)} %constant_dynamic-slice_fusion.2, f32[3,2048]{1,0:T(4,128)S(1)} %get-tuple-element.212), kind=kLoop, calls=%fused_computation.4.clone.1 | loop fusion | flops 13631488 | bytes 8443904 | tf_op jit(solution)/shard_map/while/body/eval_jaxpr/reduce_sum | solution.py:64
  251.2 31.0 %scatter_custom_fusion.1 = f32[16384]{0:T(1024)} fusion(s32[8192]{0:T(1024)S(1)} %broadcast_select_fusion, f32[8192]{0:T(1024)S(1)} %bitcast.88, f32[]{:T(128)} %constant.9.clone.1), kind=kCustom, calls=%fused_computation.253 | custom fusion | bytes 65540
  282.3 10.2 %all-to-all-start = ((f32[128,1,128]{2,1,0:T(1,128)}), f32[128,1,128]{2,1,0:T(1,128)S(1)}, u32[]{:S(2)}, u32[]{:S(2)}) async-start(f32[128,1,128]{2,1,0:T(1,128)} %bitcast.13), calls=%async_computation | async-start | bytes 131072 | tf_op jit(solution)/shard_map/all_to_all | solution.py:116
  299.5 12.5 %scatter_fusion = f32[524288]{0:T(1024)S(1)} fusion(f32[524288]{0:T(1024)S(1)} %bitcast.74, s32[2048]{0:T(1024)S(1)} %bitcast.86, f32[2048]{0:T(1024)S(1)} %bitcast.85), kind=kCustom, calls=%fused_computation | custom fusion | flops 2048 | bytes 32768 | tf_op jit(solution)/shard_map/scatter-add | solution.py:119
  317.8 11.6 %rev.12 = f32[32,128,3]{2,1,0:T(8,128)} reverse(f32[32,128,3]{2,1,0:T(8,128)S(1)} %bitcast.69), dimensions={2} | reverse | bytes 98304 | tf_op jit(solution)/shard_map/rev | solution.py:38
  389.1 17.4 %rev.13 = f32[32,128,3]{2,1,0:T(8,128)} reverse(f32[32,128,3]{2,1,0:T(8,128)} %slice.569), dimensions={2} | reverse | bytes 98304 | tf_op jit(solution)/shard_map/rev | solution.py:38
  411.9 16.5 %fusion.72 = f32[32,128,128]{2,1,0:T(8,128)} fusion(f32[32,128,128]{2,1,0:T(8,128)S(1)} %bitcast.73, f32[32,128,3]{2,1,0:T(8,128)} %broadcast_multiply_fusion.1, f32[32,128,128]{2,1,0:T(8,128)} %slice.568, f32[32,134,128]{2,1,0:T(8,128)S(1)} %maximum_bitcast_fusion.3, f32[38,134,128]{2,1,0:T(8,128)} %slice_bitcast_fusion.1), kind=kLoop, calls=%fused_computation.142 | loop fusion | flops 16252928 | bytes 31506432 | tf_op jit(solution)/shard_map/sub | solution.py:55
  434.1 14.9 %rev.14 = f32[32,128,3]{2,1,0:T(8,128)S(1)} reverse(f32[32,128,3]{2,1,0:T(8,128)} %bitcast.75), dimensions={2} | reverse | bytes 98304 | tf_op jit(solution)/shard_map/rev | solution.py:38
  457.6 8.3 %fusion.27 = (f32[1,32,128,128]{3,2,1,0:T(8,128)}, f32[1,32,128,128]{3,2,1,0:T(8,128)}) fusion(f32[32,128,128]{2,1,0:T(8,128)S(1)} %copy-done.2, f32[3,128,128]{2,1,0:T(8,128)S(1)} %collective-permute-done.9, f32[3,128,128]{2,1,0:T(8,128)S(1)} %collective-permute-done.8, f32[32,128,3]{2,1,0:T(8,128)S(1)} %broadcast_multiply_fusion.2), kind=kLoop, calls=%fused_computation.97 | loop fusion | flops 13107200 | bytes 6733824 | tf_op jit(solution)/shard_map/stack | solution.py:48
  516.0 17.4 %rev.15 = f32[32,128,3]{2,1,0:T(8,128)} reverse(f32[32,128,3]{2,1,0:T(8,128)} %slice.611), dimensions={2} | reverse | bytes 98304 | tf_op jit(solution)/shard_map/rev | solution.py:38
  540.4 20.3 %fusion.52 = f32[1,32,128,128]{3,2,1,0:T(8,128)} fusion(f32[32,128,128]{2,1,0:T(8,128)} %fusion.72, f32[32,128,3]{2,1,0:T(8,128)} %broadcast_multiply_fusion, f32[32,128,128]{2,1,0:T(8,128)} %slice.610, f32[32,134,128]{2,1,0:T(8,128)} %maximum_bitcast_fusion.2, f32[38,134,128]{2,1,0:T(8,128)} %slice_bitcast_fusion), kind=kLoop, calls=%fused_computation.122 | loop fusion | flops 16252928 | bytes 31506432 | tf_op jit(solution)/shard_map/broadcast_in_dim | solution.py:127
  (258 shorter events, 297.3 us)
Async XLA Ops:
  13.4 279.1 %copy-start.18 = (s32[1,16,128]{2,1,0:T(8,128)S(1)}, s32[1,16,128]{2,1,0:T(8,128)}, u32[]{:S(2)}) copy-start(s32[1,16,128]{2,1,0:T(8,128)} %param.18) | copy-start | bytes 24580
  282.3 17.2 %all-to-all-start = ((f32[128,1,128]{2,1,0:T(1,128)}), f32[128,1,128]{2,1,0:T(1,128)S(1)}, u32[]{:S(2)}, u32[]{:S(2)}) async-start(f32[128,1,128]{2,1,0:T(1,128)} %bitcast.13), calls=%async_computation | async-start | bytes 131072 | tf_op jit(solution)/shard_map/all_to_all | solution.py:116
  292.5 7.0 %slice-start.6 = ((f32[4,32,128,128]{3,2,1,0:T(8,128)}), f32[1,32,128,128]{3,2,1,0:T(8,128)S(1)}, s32[]{:S(2)}) async-start(f32[4,32,128,128]{3,2,1,0:T(8,128)} %param.12), calls=%async_computation.7 | async-start | bytes 4194304 | tf_op jit(solution)/shard_map/slice | solution.py:119
  312.0 19.6 %collective-permute-start = (f32[3,128,128]{2,1,0:T(8,128)S(1)}, f32[3,128,128]{2,1,0:T(8,128)S(1)}, u32[]{:S(2)}, u32[]{:S(2)}) collective-permute-start(f32[3,128,128]{2,1,0:T(8,128)S(1)} %bitcast.81), channel_id=1, source_target_pairs={{8,0},{16,8},{24,16},{32,24},{40,32},{48,40},{56,48},{64,56},{72,6... | collective-permute-start | bytes 589832 | tf_op jit(solution)/shard_map/ppermute | solution.py:22
  315.9 15.7 %collective-permute-start.1 = (f32[3,128,128]{2,1,0:T(8,128)S(1)}, f32[3,128,128]{2,1,0:T(8,128)S(1)}, u32[]{:S(2)}, u32[]{:S(2)}) collective-permute-start(f32[3,128,128]{2,1,0:T(8,128)S(1)} %bitcast.80), channel_id=1, source_target_pairs={{0,8},{8,16},{16,24},{24,32},{32,40},{40,48},{48,56},{56,64},{64,7... | collective-permute-start | bytes 589832 | tf_op jit(solution)/shard_map/ppermute | solution.py:19
  331.7 11.8 %collective-permute-start.2 = (f32[38,3,128]{2,1,0:T(4,128)S(1)}, f32[38,3,128]{2,1,0:T(4,128)S(1)}, u32[]{:S(2)}, u32[]{:S(2)}) collective-permute-start(f32[38,3,128]{2,1,0:T(4,128)S(1)} %get-tuple-element.94), channel_id=1, source_target_pairs={{1,0},{2,1},{3,2},{4,3},{5,4},{6,5},{7,6},{9,8},{10,9},{11,10},{12... | collective-permute-start | bytes 175112 | tf_op jit(solution)/shard_map/ppermute | solution.py:22
  335.4 8.1 %collective-permute-start.3 = (f32[38,3,128]{2,1,0:T(4,128)S(1)}, f32[38,3,128]{2,1,0:T(4,128)S(1)}, u32[]{:S(2)}, u32[]{:S(2)}) collective-permute-start(f32[38,3,128]{2,1,0:T(4,128)S(1)} %get-tuple-element.95), channel_id=1, source_target_pairs={{0,1},{1,2},{2,3},{3,4},{4,5},{5,6},{6,7},{8,9},{9,10},{10,11},{11... | collective-permute-start | bytes 175112 | tf_op jit(solution)/shard_map/ppermute | solution.py:19
  350.8 35.5 %copy-start.1 = (f32[3,32,128,128]{3,2,1,0:T(8,128)}, f32[3,32,128,128]{3,2,1,0:T(8,128)S(1)}, u32[]{:S(2)}) copy-start(f32[3,32,128,128]{3,2,1,0:T(8,128)S(1)} %fusion.17) | copy-start | bytes 18874372
  350.9 12.7 %collective-permute-start.4 = (f32[3,3,128,128]{3,2,1,0:T(8,128)S(1)}, f32[3,3,128,128]{3,2,1,0:T(8,128)S(1)}, u32[]{:S(2)}, u32[]{:S(2)}) collective-permute-start(f32[3,3,128,128]{3,2,1,0:T(8,128)S(1)} %get-tuple-element.86), channel_id=1, source_target_pairs={{0,8},{8,16},{16,24},{24,32},{32,40},{40,48},{48,56},{56,64},{64,7... | collective-permute-start | bytes 1769480 | tf_op jit(solution)/shard_map/ppermute | solution.py:19
  354.7 20.4 %copy-start.17 = (s32[32,128]{1,0:T(8,128)S(1)}, s32[32,128]{1,0:T(8,128)}, u32[]{:S(2)}) copy-start(s32[32,128]{1,0:T(8,128)} %param.13) | copy-start | bytes 49156
  354.7 13.6 %collective-permute-start.5 = (f32[3,3,128,128]{3,2,1,0:T(8,128)S(1)}, f32[3,3,128,128]{3,2,1,0:T(8,128)S(1)}, u32[]{:S(2)}, u32[]{:S(2)}) collective-permute-start(f32[3,3,128,128]{3,2,1,0:T(8,128)S(1)} %get-tuple-element.87), channel_id=1, source_target_pairs={{8,0},{16,8},{24,16},{32,24},{40,32},{48,40},{56,48},{64,56},{72,6... | collective-permute-start | bytes 1769480 | tf_op jit(solution)/shard_map/ppermute | solution.py:22
  368.3 10.7 %collective-permute-start.6 = (f32[3,38,3,128]{3,2,1,0:T(4,128)S(1)}, f32[3,38,3,128]{3,2,1,0:T(4,128)S(1)}, u32[]{:S(2)}, u32[]{:S(2)}) collective-permute-start(f32[3,38,3,128]{3,2,1,0:T(4,128)S(1)} %get-tuple-element.82), channel_id=1, source_target_pairs={{0,1},{1,2},{2,3},{3,4},{4,5},{5,6},{6,7},{8,9},{9,10},{10,11},{11... | collective-permute-start | bytes 525320 | tf_op jit(solution)/shard_map/ppermute | solution.py:19
  372.2 10.5 %collective-permute-start.7 = (f32[3,38,3,128]{3,2,1,0:T(4,128)S(1)}, f32[3,38,3,128]{3,2,1,0:T(4,128)S(1)}, u32[]{:S(2)}, u32[]{:S(2)}) collective-permute-start(f32[3,38,3,128]{3,2,1,0:T(4,128)S(1)} %get-tuple-element.83), channel_id=1, source_target_pairs={{1,0},{2,1},{3,2},{4,3},{5,4},{6,5},{7,6},{9,8},{10,9},{11,10},{12... | collective-permute-start | bytes 525320 | tf_op jit(solution)/shard_map/ppermute | solution.py:22
  429.4 20.2 %collective-permute-start.8 = (f32[3,128,128]{2,1,0:T(8,128)S(1)}, f32[3,128,128]{2,1,0:T(8,128)S(1)}, u32[]{:S(2)}, u32[]{:S(2)}) collective-permute-start(f32[3,128,128]{2,1,0:T(8,128)S(1)} %get-tuple-element.99), channel_id=1, source_target_pairs={{8,0},{16,8},{24,16},{32,24},{40,32},{48,40},{56,48},{64,56},{72,6... | collective-permute-start | bytes 589832 | tf_op jit(solution)/shard_map/ppermute | solution.py:22
  431.4 18.3 %collective-permute-start.9 = (f32[3,128,128]{2,1,0:T(8,128)S(1)}, f32[3,128,128]{2,1,0:T(8,128)S(1)}, u32[]{:S(2)}, u32[]{:S(2)}) collective-permute-start(f32[3,128,128]{2,1,0:T(8,128)S(1)} %get-tuple-element.98), channel_id=1, source_target_pairs={{0,8},{8,16},{16,24},{24,32},{32,40},{40,48},{48,56},{56,64},{64,7... | collective-permute-start | bytes 589832 | tf_op jit(solution)/shard_map/ppermute | solution.py:19
  450.7 15.3 %collective-permute-start.10 = (f32[38,3,128]{2,1,0:T(4,128)S(1)}, f32[38,3,128]{2,1,0:T(4,128)S(1)}, u32[]{:S(2)}, u32[]{:S(2)}) collective-permute-start(f32[38,3,128]{2,1,0:T(4,128)S(1)} %get-tuple-element.90), channel_id=1, source_target_pairs={{1,0},{2,1},{3,2},{4,3},{5,4},{6,5},{7,6},{9,8},{10,9},{11,10},{12... | collective-permute-start | bytes 175112 | tf_op jit(solution)/shard_map/ppermute | solution.py:22
  455.5 10.5 %collective-permute-start.11 = (f32[38,3,128]{2,1,0:T(4,128)S(1)}, f32[38,3,128]{2,1,0:T(4,128)S(1)}, u32[]{:S(2)}, u32[]{:S(2)}) collective-permute-start(f32[38,3,128]{2,1,0:T(4,128)S(1)} %get-tuple-element.91), channel_id=1, source_target_pairs={{0,1},{1,2},{2,3},{3,4},{4,5},{5,6},{6,7},{8,9},{9,10},{10,11},{11... | collective-permute-start | bytes 175112 | tf_op jit(solution)/shard_map/ppermute | solution.py:19
  475.0 38.2 %copy-start = (f32[3,32,128,128]{3,2,1,0:T(8,128)}, f32[3,32,128,128]{3,2,1,0:T(8,128)S(1)}, u32[]{:S(2)}) copy-start(f32[3,32,128,128]{3,2,1,0:T(8,128)S(1)} %fusion.18) | copy-start | bytes 18874372
  475.1 12.7 %collective-permute-start.12 = (f32[3,3,128,128]{3,2,1,0:T(8,128)S(1)}, f32[3,3,128,128]{3,2,1,0:T(8,128)S(1)}, u32[]{:S(2)}, u32[]{:S(2)}) collective-permute-start(f32[3,3,128,128]{3,2,1,0:T(8,128)S(1)} %get-tuple-element.84), channel_id=1, source_target_pairs={{0,8},{8,16},{16,24},{24,32},{32,40},{40,48},{48,56},{56,64},{64,7... | collective-permute-start | bytes 1769480 | tf_op jit(solution)/shard_map/ppermute | solution.py:19
  480.9 13.0 %collective-permute-start.13 = (f32[3,3,128,128]{3,2,1,0:T(8,128)S(1)}, f32[3,3,128,128]{3,2,1,0:T(8,128)S(1)}, u32[]{:S(2)}, u32[]{:S(2)}) collective-permute-start(f32[3,3,128,128]{3,2,1,0:T(8,128)S(1)} %get-tuple-element.85), channel_id=1, source_target_pairs={{8,0},{16,8},{24,16},{32,24},{40,32},{48,40},{56,48},{64,56},{72,6... | collective-permute-start | bytes 1769480 | tf_op jit(solution)/shard_map/ppermute | solution.py:22
  494.0 11.5 %collective-permute-start.14 = (f32[3,38,3,128]{3,2,1,0:T(4,128)S(1)}, f32[3,38,3,128]{3,2,1,0:T(4,128)S(1)}, u32[]{:S(2)}, u32[]{:S(2)}) collective-permute-start(f32[3,38,3,128]{3,2,1,0:T(4,128)S(1)} %get-tuple-element.80), channel_id=1, source_target_pairs={{0,1},{1,2},{2,3},{3,4},{4,5},{5,6},{6,7},{8,9},{9,10},{10,11},{11... | collective-permute-start | bytes 525320 | tf_op jit(solution)/shard_map/ppermute | solution.py:19
  498.4 11.3 %collective-permute-start.15 = (f32[3,38,3,128]{3,2,1,0:T(4,128)S(1)}, f32[3,38,3,128]{3,2,1,0:T(4,128)S(1)}, u32[]{:S(2)}, u32[]{:S(2)}) collective-permute-start(f32[3,38,3,128]{3,2,1,0:T(4,128)S(1)} %get-tuple-element.81), channel_id=1, source_target_pairs={{1,0},{2,1},{3,2},{4,3},{5,4},{6,5},{7,6},{9,8},{10,9},{11,10},{12... | collective-permute-start | bytes 525320 | tf_op jit(solution)/shard_map/ppermute | solution.py:22
  537.1 23.6 %slice-start = ((s8[6291456]{0:T(1024)(128)(4,1)}), s8[4194304]{0:T(1024)(128)(4,1)S(1)}, s32[]{:S(2)}) async-start(s8[6291456]{0:T(1024)(128)(4,1)} %bitcast.63), calls=%async_computation.1 | async-start | bytes 8388608
  540.4 20.3 %slice-start.1 = ((s8[6291456]{0:T(1024)(128)(4,1)}), s8[2097152]{0:T(1024)(128)(4,1)S(1)}, s32[]{:S(2)}) async-start(s8[6291456]{0:T(1024)(128)(4,1)} %bitcast.63), calls=%async_computation.2 | async-start | bytes 4194304
  (20 other events, 60.4 us)
where the time goes:
time: 575 us; the launch traced here: 566 us
  other arithmetic  272 us (47%)
  local copies, waits for them, and re-layouts  141 us (25%)
  starting transfers between devices  62 us (11%)
  waiting for transfers between devices  43.8 us (8%)
  matrix products  35.8 us (6%)
  loops' own time  11.3 us (2%)
    reduce_sum x16, other arithmetic, panel_kernel(): distance_sq = jnp.sum(offset * offset, axis=0) + SOFTENING  119 us
    rev x4, local copies, waits for them, and re-layouts, ground_pad(): mirror_cells = parity * ground_flags[:, :, None] * grid_field[:, :, 2::-1]  61.3 us
    unnamed x55, local copies, waits for them, and re-layouts  43.3 us
    dot_general x16, matrix products, observed_values(): history = jnp.dot(kernel, source_matrix, preferred_element_type=jnp.float32)  35.8 us
    another operation x19, other arithmetic  29.2 us
    ppermute x8, starting transfers between devices, padded(): lax.ppermute(lax.slice_in_dim(block, block.shape[dim] - width, None, axis...  26.6 us
    ppermute x8, starting transfers between devices, padded(): lax.ppermute(lax.slice_in_dim(block, 0, width, axis=dim), axis, backward)  25.2 us
    broadcast_in_dim x1, other arithmetic, body(): return jnp.concatenate([pressure[None], velocity], axis=0)  20.3 us
  transfers between devices with their start and end apart: 17, of which 9 were waited for; matrix products, arithmetic and copies ran while one was open for 8% of the time, Pallas kernels for 0%

commit v1 on v0

v1 whole, which is shorter than its diff:
```python
import functools

import jax
import jax.numpy as jnp
from jax import lax
from jax.experimental import pallas as pl
from jax.experimental.pallas import tpu as pltpu
from jax.sharding import PartitionSpec as P

BF = jnp.bfloat16
F32 = jnp.float32
MESH = pl.DeviceIdType.MESH
WEIGHTS = (0.770882380518, -0.166705904415, 0.02084314277)
DT = 0.5
SOFTENING = 0.01
REACH = 3
WIDE = 6
PAD = 8
FEATURES = 80
MERGE = False


def split3(x):
    a = x.astype(BF).astype(F32)
    r = x - a
    b = r.astype(BF).astype(F32)
    return a, b, r - b


def dot(a, b):
    return jnp.dot(a, b, preferred_element_type=F32)


def dot_nt(a, b):
    return lax.dot_general(a, b, (((1,), (1,)), ((), ())), preferred_element_type=F32)


def panel_scratch(m, q, devices):
    return [
        pltpu.VMEM((8, m), F32),
        pltpu.VMEM((8, q), F32),
        pltpu.VMEM((2, q, FEATURES), BF),
        pltpu.VMEM((3 * devices, 128), F32),
        pltpu.VMEM((devices, 128), F32),
    ]


def panel_part(nbx, nby, obs, slots, fracs, owners, pts, nrm, src, packet, eo, ep, feat, pieces, base):
    m = obs.shape[1]
    q = pts.shape[1]
    samples = src.shape[1]
    devices = nbx * nby
    tile = min(1024, m)
    chunk = min(512, q)
    sub = 256

    o = obs[...]
    eo[0:3, :] = o
    eo[3:4, :] = jnp.sum(o * o, axis=0, keepdims=True)
    eo[4:5, :] = jnp.ones((1, m), F32)
    eo[5:8, :] = jnp.zeros((3, m), F32)
    p = pts[...]
    n = nrm[...]

    def lay(k):
        s = split3(ep[...])
        rows = [s[0], s[1], s[2]] * 3 + [jnp.zeros_like(s[0])]
        table = jnp.concatenate(rows + [jnp.zeros((128 - FEATURES, q), F32)], axis=0)
        feat[k] = table.T[:, :FEATURES].astype(BF)

    ep[0:3, :] = -2.0 * p
    ep[3:4, :] = jnp.ones((1, q), F32)
    ep[4:5, :] = jnp.sum(p * p, axis=0, keepdims=True) + SOFTENING
    ep[5:8, :] = jnp.zeros((3, q), F32)
    lay(0)
    ep[0:3, :] = n
    ep[3:4, :] = jnp.zeros((1, q), F32)
    ep[4:5, :] = -jnp.sum(p * n, axis=0, keepdims=True)
    lay(1)
    pieces[...] = jnp.zeros_like(pieces)
    base[...] = jnp.zeros_like(base)
    row = lax.broadcasted_iota(jnp.int32, (devices, 1), 0)
    row_owner = (row % nbx) * nby + row // nbx
    before = (
        lax.broadcasted_iota(jnp.int32, (sub, sub), 0) < lax.broadcasted_iota(jnp.int32, (sub, sub), 1)
    ).astype(F32).astype(BF)
    ranks = lax.broadcasted_iota(jnp.int32, (128, 1), 0).astype(F32)
    times = lax.broadcasted_iota(jnp.int32, (samples, 1), 0)

    def one_tile(t, carry):
        o0 = pl.multiple_of(t * tile, tile)
        here = pl.ds(o0, tile)
        e = split3(eo[:, here])
        of = jnp.concatenate(
            [e[0]] * 3 + [e[1]] * 3 + [e[2]] * 3 + [jnp.zeros_like(e[0])], axis=0
        ).astype(BF)

        def one_chunk(c, acc):
            q0 = pl.multiple_of(c * chunk, chunk)
            rows = pl.ds(q0, chunk)
            inverse = lax.rsqrt(dot(feat[0, rows, :], of))
            near = dot(feat[1, rows, :], of) * inverse * inverse
            far = near * inverse
            acc = acc + dot(src[0, :, rows], inverse.astype(BF))
            acc = acc + dot(src[1, :, rows], near.astype(BF))
            return acc + dot(src[2, :, rows], far.astype(BF))

        history = lax.fori_loop(0, q // chunk, one_chunk, jnp.zeros((samples, tile), F32))
        slot = slots[:, here]
        frac = fracs[:, here]
        weights = jnp.where(times == slot, 1.0 - frac, 0.0) + jnp.where(times == slot + 1, frac, 0.0)
        value = jnp.sum(history * weights, axis=0, keepdims=True)
        parts = split3(value)
        owner = owners[:, here]
        for s in range(tile // sub):
            cut = slice(s * sub, (s + 1) * sub)
            mine = owner[:, cut] == row_owner
            hot = jnp.where(mine, 1.0, 0.0)
            earlier = dot(hot.astype(BF), before) + base[:, 0:1]
            rank = jnp.sum(hot * earlier, axis=0, keepdims=True)
            base[...] += jnp.sum(hot, axis=1, keepdims=True)
            at_rank = jnp.where(rank == ranks, 1.0, 0.0).astype(BF)
            loads = jnp.concatenate([jnp.where(mine, v[:, cut], 0.0) for v in parts], axis=0).astype(BF)
            pieces[...] += dot_nt(loads, at_rank)
        return carry

    lax.fori_loop(0, m // tile, one_tile, 0)
    packet[...] = pieces[0:devices, :] + pieces[devices:2 * devices, :] + pieces[2 * devices:, :]


def panel_kernel(nbx, nby, *refs):
    panel_part(nbx, nby, *refs)


def box_kernel(nbx, nby, packet, cells, ground, fields, out, pa, pb, us, vs, ws, flags, zmat, hot_own, hot_lr, hot_du, bt,
               gathered, agg, arrived, passed, passed_cells, load_sem, raw_send, raw_recv, one_send, one_recv,
               two_send, two_recv, nb_send, nb_recv, rim_send, rim_recv, out_sem):
    bx = lax.axis_index("bx")
    by = lax.axis_index("by")
    gx, gy, gz = fields.shape[1:]
    arrivals = nbx * 128
    has = (bx > 0, bx < nbx - 1, by > 0, by < nby - 1)
    to = (
        (jnp.maximum(bx - 1, 0), by),
        (jnp.minimum(bx + 1, nbx - 1), by),
        (bx, jnp.maximum(by - 1, 0)),
        (bx, jnp.minimum(by + 1, nby - 1)),
    )
    back = (1, 0, 3, 2)

    barrier = pltpu.get_barrier_semaphore()
    for i in range(1, nby):
        pl.semaphore_signal(barrier, inc=1, device_id=(bx, lax.rem(by + i, nby)), device_id_type=MESH)
    for i in range(1, nbx):
        pl.semaphore_signal(barrier, inc=1, device_id=(lax.rem(bx + i, nbx), by), device_id_type=MESH)
    pl.semaphore_wait(barrier, nby - 1 + nbx - 1)

    def remote(src, dst, send, recv, target):
        return pltpu.make_async_remote_copy(
            src_ref=src, dst_ref=dst, send_sem=send, recv_sem=recv, device_id=target, device_id_type=MESH
        )

    firsts = []
    for i in range(1, nby):
        peer = lax.rem(by + i, nby)
        rows = pl.ds(pl.multiple_of(peer * nbx, nbx), nbx)
        copy = remote(packet.at[rows, :], gathered.at[i], one_send.at[i], one_recv.at[i], (bx, peer))
        copy.start()
        firsts.append(copy)

    x_core = pl.ds(WIDE, gx)
    y_core = pl.ds(PAD, gy)
    give_p = (
        fields.at[0, pl.ds(0, WIDE)],
        fields.at[0, pl.ds(gx - WIDE, WIDE)],
        fields.at[0, :, pl.ds(0, PAD)],
        fields.at[0, :, pl.ds(gy - PAD, PAD)],
    )
    give_v = (
        fields.at[1, pl.ds(0, REACH)],
        fields.at[1, pl.ds(gx - REACH, REACH)],
        fields.at[2, :, pl.ds(0, PAD)],
        fields.at[2, :, pl.ds(gy - PAD, PAD)],
    )

    def rim(ref):
        return (
            ref.at[pl.ds(0, WIDE), y_core],
            ref.at[pl.ds(WIDE + gx, WIDE), y_core],
            ref.at[x_core, pl.ds(0, PAD)],
            ref.at[x_core, pl.ds(PAD + gy, PAD)],
        )

    rim_a = rim(pa)
    rim_b = rim(pb)
    rim_v = (
        us.at[pl.ds(0, REACH)],
        us.at[pl.ds(REACH + gx, REACH)],
        vs.at[:, pl.ds(0, PAD)],
        vs.at[:, pl.ds(PAD + gy, PAD)],
    )

    raw = []
    for s in range(4):
        raw.append((
            remote(cells.at[0], passed_cells.at[back[s]], raw_send.at[s], raw_recv.at[s], to[s]),
            remote(give_p[s], rim_a[back[s]], raw_send.at[4 + s], raw_recv.at[4 + s], to[s]),
            remote(give_v[s], rim_v[back[s]], raw_send.at[8 + s], raw_recv.at[8 + s], to[s]),
        ))

    def landed(src, dst, recv, s):
        return remote(src, dst, raw_send.at[s], recv, to[s % 4])

    for s in range(4):
        @pl.when(has[s])
        def _(s=s):
            for copy in raw[s]:
                copy.start()

    loads = [
        pltpu.make_async_copy(fields.at[0], pa.at[x_core, y_core], load_sem.at[0]),
        pltpu.make_async_copy(fields.at[1], us.at[pl.ds(REACH, gx)], load_sem.at[1]),
        pltpu.make_async_copy(fields.at[2], vs.at[:, y_core], load_sem.at[2]),
        pltpu.make_async_copy(fields.at[3], ws, load_sem.at[3]),
    ]
    for copy in loads:
        copy.start()

    for s in range(4):
        @pl.when(jnp.logical_not(has[s]))
        def _(s=s):
            rim_a[s][...] = jnp.zeros(rim_a[s].shape, F32)
            rim_b[s][...] = jnp.zeros(rim_b[s].shape, F32)
            rim_v[s][...] = jnp.zeros(rim_v[s].shape, F32)

    scaled = [DT * w for w in WEIGHTS]
    source = lax.broadcasted_iota(jnp.int32, (gz, 2 * gz), 0)
    column = lax.broadcasted_iota(jnp.int32, (gz, 2 * gz), 1)
    difference = jnp.zeros((gz, 2 * gz), F32)
    for j, w in enumerate(scaled, 1):
        difference = jnp.where(jnp.logical_and(column < gz, source - column == j), w, difference)
        difference = jnp.where(jnp.logical_and(column < gz, column - source == j), -w, difference)
        difference = jnp.where(jnp.logical_and(column >= gz, source + column - gz + 1 == j), -w, difference)
    coarse = difference.astype(BF)
    zmat[0:gz, :] = coarse
    zmat[gz:2 * gz, :] = coarse
    zmat[2 * gz:, :] = (difference - coarse.astype(F32)).astype(BF)

    ground_t = ground[...].astype(F32).T
    for x in range(gx):
        flags[x] = jnp.broadcast_to(ground_t[:, x:x + 1], (gy, gz))

    def fill(ref, rows, row_id):
        step = min(256, rows)

        def go(i, carry):
            r0 = pl.multiple_of(i * step, step)
            ids = lax.broadcasted_iota(jnp.int32, (step, 1), 0) + r0
            for b in range(nbx):
                ref[pl.ds(r0, step), b * 128:(b + 1) * 128] = jnp.where(
                    ids == row_id[b:b + 1, :], 1.0, 0.0
                ).astype(BF)
            return carry

        lax.fori_loop(0, rows // step, go, 0)

    fill(hot_own, gx * gy, cells[0] // gz)

    for copy in firsts:
        copy.wait_recv()
    mine = pl.ds(pl.multiple_of(by * nbx, nbx), nbx)
    total = packet[mine, :]
    for i in range(1, nby):
        total = total + gathered[i]
    for i in range(nbx):
        agg[i] = total[i:i + 1, :]
    seconds = []
    for i in range(1, nbx):
        peer = lax.rem(bx + i, nbx)
        copy = remote(agg.at[peer], arrived.at[bx], two_send.at[i], two_recv.at[i], (peer, by))
        copy.start()
        seconds.append(copy)
    arrived[bx] = agg[bx]

    cells_in = []
    for s in range(4):
        @pl.when(has[s])
        def _(s=s):
            landed(cells.at[0], passed_cells.at[s], raw_recv.at[back[s]], s).wait_recv()
            row_id = passed_cells[s] // gz
            if s == 0:
                fill(hot_lr.at[0], WIDE * gy, row_id - (gx - WIDE) * gy)
            elif s == 1:
                fill(hot_lr.at[1], WIDE * gy, row_id)
            else:
                y = row_id % gy - (gy - PAD if s == 2 else 0)
                inside = jnp.logical_and(y >= 0, y < PAD)
                fill(hot_du.at[s - 2], gx * PAD, jnp.where(inside, row_id // gy * PAD + y, -1))

    heights = lax.broadcasted_iota(jnp.int32, (gz, 1), 0)

    def targets(values, cell_rows):
        for b in range(nbx):
            v = values(b)
            at = heights == cell_rows[b:b + 1, :] % gz
            hi = v.astype(BF).astype(F32)
            bt[0:gz, b * 128:(b + 1) * 128] = jnp.where(at, hi, 0.0).astype(BF)
            bt[gz:2 * gz, b * 128:(b + 1) * 128] = jnp.where(at, v - hi, 0.0).astype(BF)

    def added(hot):
        both = dot_nt(hot, bt[...])
        return both[:, :gz] + both[:, gz:]

    for copy in seconds:
        copy.wait_recv()
    handed = [
        remote(arrived, passed.at[back[s]], nb_send.at[s], nb_recv.at[s], to[s]) for s in range(4)
    ]
    for s in range(4):
        @pl.when(has[s])
        def _(s=s):
            handed[s].start()

    targets(lambda b: arrived[b], cells[0])
    loads[0].wait()
    planes = 4

    def inject_own(i, carry):
        r0 = pl.multiple_of(i * planes * gy, planes * gy)
        extra = added(hot_own[pl.ds(r0, planes * gy), :]).reshape(planes, gy, gz)
        pa[pl.ds(WIDE + i * planes, planes), PAD:PAD + gy, :] += extra
        return carry

    lax.fori_loop(0, gx // planes, inject_own, 0)

    for s in range(4):
        @pl.when(has[s])
        def _(s=s):
            landed(give_p[s], rim_a[s], raw_recv.at[4 + back[s]], 4 + s).wait_recv()
            landed(give_v[s], rim_v[s], raw_recv.at[8 + back[s]], 8 + s).wait_recv()
            remote(arrived, passed.at[s], nb_send.at[s], nb_recv.at[back[s]], to[s]).wait_recv()
            targets(lambda b: passed[s, b], passed_cells[s])
            if s < 2:
                x0 = 0 if s == 0 else WIDE + gx

                def inject_x(i, carry):
                    r0 = pl.multiple_of(i * gy, gy)
                    pa[x0 + i, PAD:PAD + gy, :] += added(hot_lr[s, pl.ds(r0, gy), :])
                    return carry

                lax.fori_loop(0, WIDE, inject_x, 0)
            else:
                y0 = 0 if s == 2 else PAD + gy
                pa[WIDE:WIDE + gx, y0:y0 + PAD, :] += added(hot_du[s - 2]).reshape(gx, PAD, gz)

    for copy in loads[1:]:
        copy.wait()

    def z_term(f, flag):
        high = f.astype(BF)
        low = (f - high.astype(F32)).astype(BF)
        both = dot(jnp.concatenate([high, low, high], axis=1), zmat[...])
        return both[:, :gz] + flag * both[:, gz:]

    def span(get):
        total = None
        for j, w in enumerate(scaled, 1):
            term = w * (get(j) - get(-j))
            total = term if total is None else total + term
        return total

    def loop(lo, hi, step):
        def go(i, carry):
            step(i)
            return carry

        lax.fori_loop(lo, hi, go, 0)

    def u_plane(p, i):
        us[i] = us[i] - span(lambda j: p[i + REACH + j, PAD:PAD + gy, :])

    def v_rows(p, x, lo, hi):
        vs[x, lo:hi, :] = vs[x, lo:hi, :] - span(lambda j: p[x + WIDE, lo + j:hi + j, :])

    def w_plane(p, x):
        ws[x] = ws[x] - z_term(p[x + WIDE, PAD:PAD + gy, :], flags[x])

    def p_rows(old, new, x, lo, hi):
        change = span(lambda j: us[x + REACH + j, lo:hi, :])
        change = change + span(lambda j: vs[x, PAD + lo + j:PAD + hi + j, :])
        change = change + z_term(ws[x, lo:hi, :], -flags[x, lo:hi, :])
        new[x + WIDE, PAD + lo:PAD + hi, :] = old[x + WIDE, PAD + lo:PAD + hi, :] - change

    def outer_u(p, s):
        lo = 0 if s == 0 else REACH + gx

        @pl.when(has[s])
        def _():
            loop(lo, lo + REACH, lambda i: u_plane(p, i))

    def outer_v(p, s):
        lo = PAD - REACH if s == 2 else PAD + gy

        @pl.when(has[s])
        def _():
            loop(0, gx, lambda x: v_rows(p, x, lo, lo + REACH))

    for s in (0, 1):
        outer_u(pa, s)
    for s in (2, 3):
        outer_v(pa, s)

    def first_velocity(x):
        u_plane(pa, x + REACH)
        v_rows(pa, x, PAD, PAD + gy)
        w_plane(pa, x)

    loop(0, gx, first_velocity)

    give_b = (
        pb.at[pl.ds(WIDE, WIDE), y_core],
        pb.at[pl.ds(gx, WIDE), y_core],
        pb.at[x_core, pl.ds(PAD, PAD)],
        pb.at[x_core, pl.ds(gy, PAD)],
    )
    second_rim = [
        remote(give_b[s], rim_b[back[s]], rim_send.at[s], rim_recv.at[s], to[s]) for s in range(4)
    ]

    def send_rim(s):
        @pl.when(has[s])
        def _():
            second_rim[s].start()

    loop(0, WIDE, lambda x: p_rows(pa, pb, x, 0, gy))
    send_rim(0)
    loop(gx - WIDE, gx, lambda x: p_rows(pa, pb, x, 0, gy))
    send_rim(1)

    def edges(x):
        p_rows(pa, pb, x, 0, PAD)
        p_rows(pa, pb, x, gy - PAD, gy)

    loop(WIDE, gx - WIDE, edges)
    send_rim(2)
    send_rim(3)
    loop(WIDE, gx - WIDE, lambda x: p_rows(pa, pb, x, PAD, gy - PAD))

    def inner_velocity(x):
        v_rows(pb, x, 2 * PAD, gy)
        w_plane(pb, x)

    loop(0, gx, inner_velocity)
    loop(2 * REACH, gx, lambda i: u_plane(pb, i))
    outs = [
        pltpu.make_async_copy(pa.at[x_core, y_core], out.at[0], out_sem.at[0]),
        pltpu.make_async_copy(us.at[pl.ds(REACH, gx)], out.at[1], out_sem.at[1]),
        pltpu.make_async_copy(vs.at[:, y_core], out.at[2], out_sem.at[2]),
        pltpu.make_async_copy(ws, out.at[3], out_sem.at[3]),
    ]
    outs[3].start()
    for s in range(4):
        @pl.when(has[s])
        def _(s=s):
            remote(give_b[s], rim_b[s], rim_send.at[s], rim_recv.at[back[s]], to[s]).wait_recv()
    for s in (0, 1):
        outer_u(pb, s)
    loop(REACH, 2 * REACH, lambda i: u_plane(pb, i))
    loop(gx, gx + REACH, lambda i: u_plane(pb, i))
    outs[1].start()
    for s in (2, 3):
        outer_v(pb, s)

    def outer_rows(x):
        v_rows(pb, x, PAD, 2 * PAD)
        v_rows(pb, x, gy, gy + PAD)

    loop(0, gx, outer_rows)
    outs[2].start()
    loop(0, gx, lambda x: p_rows(pb, pa, x, 0, gy))
    outs[0].start()

    for copy in firsts + seconds:
        copy.wait_send()
    for s in range(4):
        @pl.when(has[s])
        def _(s=s):
            for copy in raw[s]:
                copy.wait_send()
            handed[s].wait_send()
            second_rim[s].wait_send()
    for copy in outs:
        copy.wait()


def vmem():
    return pl.BlockSpec(memory_space=pltpu.VMEM)


def anywhere():
    return pl.BlockSpec(memory_space=pl.ANY)


def body(nbx, nby, fields, ground, observers, slots, fractions, owners, arrival_cell, panel_points, panel_normals,
         sources):
    devices = nbx * nby
    m = observers.shape[1]
    q = panel_points.shape[1]
    gx, gy, gz = fields.shape[1:]
    k = nbx * 128
    packet = pl.pallas_call(
        functools.partial(panel_kernel, nbx, nby),
        out_shape=jax.ShapeDtypeStruct((devices, 128), F32),
        in_specs=[vmem()] * 7,
        out_specs=vmem(),
        scratch_shapes=panel_scratch(m, q, devices),
        compiler_params=pltpu.CompilerParams(vmem_limit_bytes=48 << 20),
        name="panels",
    )(
        observers,
        slots.reshape(1, m),
        fractions.reshape(1, m),
        owners.reshape(1, m),
        panel_points,
        panel_normals,
        sources.transpose(0, 2, 1),
    )
    dma = pltpu.SemaphoreType.DMA
    return pl.pallas_call(
        functools.partial(box_kernel, nbx, nby),
        out_shape=jax.ShapeDtypeStruct(fields.shape, F32),
        in_specs=[vmem(), vmem(), vmem(), anywhere()],
        out_specs=anywhere(),
        scratch_shapes=[
            pltpu.VMEM((gx + 2 * WIDE, gy + 2 * PAD, gz), F32),
            pltpu.VMEM((gx + 2 * WIDE, gy + 2 * PAD, gz), F32),
            pltpu.VMEM((gx + 2 * REACH, gy, gz), F32),
            pltpu.VMEM((gx, gy + 2 * PAD, gz), F32),
            pltpu.VMEM((gx, gy, gz), F32),
            pltpu.VMEM((gx, gy, gz), F32),
            pltpu.VMEM((3 * gz, 2 * gz), BF),
            pltpu.VMEM((gx * gy, k), BF),
            pltpu.VMEM((2, WIDE * gy, k), BF),
            pltpu.VMEM((2, gx * PAD, k), BF),
            pltpu.VMEM((2 * gz, k), BF),
            pltpu.VMEM((nby, nbx, 128), F32),
            pltpu.VMEM((nbx, 1, 128), F32),
            pltpu.VMEM((nbx, 1, 128), F32),
            pltpu.VMEM((4, nbx, 1, 128), F32),
            pltpu.VMEM((4, nbx, 128), jnp.int32),
            dma((4,)),
            dma((12,)),
            dma((12,)),
            dma((nby,)),
            dma((nby,)),
            dma((nbx,)),
            dma((nbx,)),
            dma((4,)),
            dma((4,)),
            dma((4,)),
            dma((4,)),
            dma((4,)),
        ],
        compiler_params=pltpu.CompilerParams(
            collective_id=0, has_side_effects=True, vmem_limit_bytes=56 << 20
        ),
        name="box",
    )(packet, arrival_cell, ground, fields)


def solution(mesh):
    placed = (
        P(None, "bx", "by", None),
        P("bx", "by"),
        P(None, "bx"),
        P("bx"),
        P("bx"),
        P("bx", None),
        P(("bx", "by"), None, None),
        P(None, "by"),
        P(None, "by"),
        P(None, "by", None),
    )
    return jax.shard_map(
        functools.partial(body, mesh.shape["bx"], mesh.shape["by"]),
        mesh=mesh,
        in_specs=placed,
        out_specs=P(None, "bx", "by", None),
        check_vma=False,
    )
```

time: 575 us -> 149 us (0.26); the launches traced: 566 us -> 147 us
  other arithmetic: 272 us -> 0 us
  Pallas kernels: 0 us -> 133 us
  local copies, waits for them, and re-layouts: 141 us -> 14.3 us
  starting transfers between devices: 62 us -> 0 us
  waiting for transfers between devices: 43.8 us -> 0 us
  matrix products: 35.8 us -> 0 us
  loops' own time: 11.3 us -> 0 us
    pallas_call x0 -> x2, Pallas kernels: none -> 133 us  [the longest x1 83.3 us: body(): pl.pallas_call(functools.partial(box_kernel, nbx, nby), out_shape=jax.Sha...]
    reduce_sum x18 -> x0, other arithmetic: 122 us -> none  [the longest x16 119 us: panel_kernel(): distance_sq = jnp.sum(offset * offset, axis=0) + SOFTENING]
    rev x4 -> x0, local copies, waits for them, and re-layouts: 61.3 us -> none  [ground_pad(): mirror_cells = parity * ground_flags[:, :, None] * grid_field[:, :, 2::-1]]
    ppermute x16 -> x0, starting transfers between devices: 51.8 us -> none  [the longest x8 26.6 us: padded(): lax.ppermute(lax.slice_in_dim(block, block.shape[dim] - width, None, axis...]
    another operation x23 -> x0, other arithmetic: 46 us -> none
    ppermute x16 -> x0, waiting for transfers between devices: 37.6 us -> none  [the longest x8 18.9 us: padded(): lax.ppermute(lax.slice_in_dim(block, block.shape[dim] - width, None, axis...]
    dot_general x16 -> x0, matrix products: 35.8 us -> none  [observed_values(): history = jnp.dot(kernel, source_matrix, preferred_element_type=jnp.float32)]
    sub x20 -> x0, other arithmetic: 34.1 us -> none  [the longest x1 16.5 us: pressure_update(): return pressure - TIME_STEP * (div_x + div_y + div_z)]
  transfers between devices with their start and end apart: 17 -> 0, of which waited for: 9 -> 0; matrix products, arithmetic and copies ran while one was open for 8% -> 0% of each run, Pallas kernels for 0% -> 0%
where the time goes in v1:
time: 149 us; the launch traced here: 147 us
  Pallas kernels  133 us (89%)
  local copies, waits for them, and re-layouts  14.3 us (10%)
    pallas_call x1, Pallas kernels, body(): pl.pallas_call(functools.partial(box_kernel, nbx, nby), out_shape=jax.Sha...  83.3 us
    pallas_call x1, Pallas kernels, body(): pl.pallas_call(functools.partial(panel_kernel, nbx, nby), out_shape=jax.S...  49.5 us
    unnamed x17, local copies, waits for them, and re-layouts  14.3 us

profile of v1, /device:TPU:36, one launch (start us, length us, event | category | flops | bytes accessed | tf_op | source)
XLA Modules:
  0.0 147.2 jit_solution(11043609001859440209)
XLA Ops:
  0.0 0.0 copy-start
  0.0 1.1 copy-done
  1.1 0.0 copy-start.2
  1.1 0.9 copy-done.2
  2.0 0.0 copy-start.3
  2.0 0.8 copy-done.3
  2.8 0.0 copy-start.4
  2.8 0.8 copy-done.4
  3.6 0.0 copy-start.5
  3.6 0.8 copy-done.5
  4.3 0.0 copy-start.6
  4.3 0.8 copy-done.6
  5.1 0.0 copy-start.7
  5.1 0.8 copy-done.7
  5.8 49.5 %panels.1.packet = f32[128,128]{1,0:T(8,128)S(1)} custom-call(f32[3,8192]{1,0:T(4,128)S(1)} %copy-done.2, s32[1,8192]{1,0:T(1,128)S(1)} %bitcast.5, f32[1,8192]{1,0:T(1,128)S(1)} %bitcast.6, s32[1,8192]{1,0:T(1,128)S(1)} %bitcast.7, f32[3,2048]{1,0:T(4,128)S(1)} %copy-done.6, f32[3,2048]{1,0:T(4,128)S(1)} %copy-done.7, bf16[3,64,2048]{2,1,0:T(8,128)(2,1)S(1)} %bitcast.4), custom_call_target="tpu_custom_call" | custom-call | tf_op jit(solution)/shard_map/panels/pallas_call | solution.py:511
  55.3 0.0 copy-start.1
  55.3 0.6 copy-done.1
  56.0 83.3 %box.1 = f32[4,32,128,128]{3,2,1,0:T(8,128)} custom-call(f32[128,128]{1,0:T(8,128)} %copy-done.1, s32[1,16,128]{2,1,0:T(8,128)} %cells.1, s32[32,128]{1,0:T(8,128)} %ground.1, f32[4,32,128,128]{3,2,1,0:T(8,128)} %fields.1), custom_call_target="tpu_custom_call" | custom-call | tf_op jit(solution)/shard_map/box/pallas_call | solution.py:529
  139.3 7.9 %copy.12 = f32[4,32,128,128]{3,2,1,0:T(8,128)} copy(f32[4,32,128,128]{3,2,1,0:T(8,128)} %box.1) | data formatting | bytes 16777216
Async XLA Ops:
  0.0 1.1 copy-start
  1.1 0.9 copy-start.2
  2.0 0.8 copy-start.3
  2.8 0.8 copy-start.4
  3.6 0.8 copy-start.5
  4.3 0.8 copy-start.6
  5.1 0.8 copy-start.7
  55.3 0.6 copy-start.1

commit v2 on v1

--- a/solution.py
+++ b/solution.py
@@ -17,7 +17,6 @@
 WIDE = 6
 PAD = 8
 FEATURES = 80
-MERGE = False
 
 
 def split3(x):
@@ -112,29 +111,31 @@
         value = jnp.sum(history * weights, axis=0, keepdims=True)
         parts = split3(value)
         owner = owners[:, here]
+        mine = owner == row_owner
+        hot = jnp.where(mine, 1.0, 0.0)
+        seen = base[...]
+        ranks_here = []
         for s in range(tile // sub):
-            cut = slice(s * sub, (s + 1) * sub)
-            mine = owner[:, cut] == row_owner
-            hot = jnp.where(mine, 1.0, 0.0)
-            earlier = dot(hot.astype(BF), before) + base[:, 0:1]
-            rank = jnp.sum(hot * earlier, axis=0, keepdims=True)
-            base[...] += jnp.sum(hot, axis=1, keepdims=True)
-            at_rank = jnp.where(rank == ranks, 1.0, 0.0).astype(BF)
-            loads = jnp.concatenate([jnp.where(mine, v[:, cut], 0.0) for v in parts], axis=0).astype(BF)
-            pieces[...] += dot_nt(loads, at_rank)
+            part = hot[:, s * sub:(s + 1) * sub]
+            earlier = dot(part.astype(BF), before) + seen[:, 0:1]
+            ranks_here.append(jnp.sum(part * earlier, axis=0, keepdims=True))
+            seen = seen + jnp.sum(part, axis=1, keepdims=True)
+        base[...] = seen
+        rank = jnp.concatenate(ranks_here, axis=1)
+        at_rank = jnp.where(rank == ranks, 1.0, 0.0).astype(BF)
+        loads = jnp.concatenate([jnp.where(mine, v, 0.0) for v in parts], axis=0).astype(BF)
+        pieces[...] += dot_nt(loads, at_rank)
         return carry
 
     lax.fori_loop(0, m // tile, one_tile, 0)
     packet[...] = pieces[0:devices, :] + pieces[devices:2 * devices, :] + pieces[2 * devices:, :]
 
 
-def panel_kernel(nbx, nby, *refs):
-    panel_part(nbx, nby, *refs)
-
-
-def box_kernel(nbx, nby, packet, cells, ground, fields, out, pa, pb, us, vs, ws, flags, zmat, hot_own, hot_lr, hot_du, bt,
-               gathered, agg, arrived, passed, passed_cells, load_sem, raw_send, raw_recv, one_send, one_recv,
-               two_send, two_recv, nb_send, nb_recv, rim_send, rim_recv, out_sem):
+def box_kernel(nbx, nby, obs_in, slots_in, fracs_in, owners_in, pts_in, nrm_in, src_in, cells_in, ground_in, fields,
+               pz, us, vs, ws, pa, pb, flags, zmat, hot_own, hot_lr, hot_du, bt,
+               gathered, agg, arrived, passed, passed_cells, obs, slots, fracs, owners, pts, nrm, src, cells, ground,
+               packet, eo, ep, feat, pieces, base, in_sem, load_sem, raw_send, raw_recv, one_send, one_recv,
+               two_send, two_recv, nb_send, nb_recv, rim_send, rim_recv):
     bx = lax.axis_index("bx")
     by = lax.axis_index("by")
     gx, gy, gz = fields.shape[1:]
@@ -148,6 +149,15 @@
     )
     back = (1, 0, 3, 2)
 
+    fetched = [
+        pltpu.make_async_copy(a, b, in_sem.at[i])
+        for i, (a, b) in enumerate((
+            (cells_in.at[0], cells), (ground_in, ground), (src_in, src), (obs_in, obs), (slots_in, slots),
+            (fracs_in, fracs), (owners_in, owners), (pts_in, pts), (nrm_in, nrm),
+        ))
+    ]
+    for copy in fetched:
+        copy.start()
     barrier = pltpu.get_barrier_semaphore()
     for i in range(1, nby):
         pl.semaphore_signal(barrier, inc=1, device_id=(bx, lax.rem(by + i, nby)), device_id_type=MESH)
@@ -159,14 +169,6 @@
         return pltpu.make_async_remote_copy(
             src_ref=src, dst_ref=dst, send_sem=send, recv_sem=recv, device_id=target, device_id_type=MESH
         )
-
-    firsts = []
-    for i in range(1, nby):
-        peer = lax.rem(by + i, nby)
-        rows = pl.ds(pl.multiple_of(peer * nbx, nbx), nbx)
-        copy = remote(packet.at[rows, :], gathered.at[i], one_send.at[i], one_recv.at[i], (bx, peer))
-        copy.start()
-        firsts.append(copy)
 
     x_core = pl.ds(WIDE, gx)
     y_core = pl.ds(PAD, gy)
@@ -203,7 +205,7 @@
     raw = []
     for s in range(4):
         raw.append((
-            remote(cells.at[0], passed_cells.at[back[s]], raw_send.at[s], raw_recv.at[s], to[s]),
+            remote(cells_in.at[0], passed_cells.at[back[s]], raw_send.at[s], raw_recv.at[s], to[s]),
             remote(give_p[s], rim_a[back[s]], raw_send.at[4 + s], raw_recv.at[4 + s], to[s]),
             remote(give_v[s], rim_v[back[s]], raw_send.at[8 + s], raw_recv.at[8 + s], to[s]),
         ))
@@ -246,9 +248,20 @@
     zmat[gz:2 * gz, :] = coarse
     zmat[2 * gz:, :] = (difference - coarse.astype(F32)).astype(BF)
 
+    for copy in fetched:
+        copy.wait()
     ground_t = ground[...].astype(F32).T
     for x in range(gx):
         flags[x] = jnp.broadcast_to(ground_t[:, x:x + 1], (gy, gz))
+
+    panel_part(nbx, nby, obs, slots, fracs, owners, pts, nrm, src, packet, eo, ep, feat, pieces, base)
+    firsts = []
+    for i in range(1, nby):
+        peer = lax.rem(by + i, nby)
+        rows = pl.ds(pl.multiple_of(peer * nbx, nbx), nbx)
+        copy = remote(packet.at[rows, :], gathered.at[i], one_send.at[i], one_recv.at[i], (bx, peer))
+        copy.start()
+        firsts.append(copy)
 
     def fill(ref, rows, row_id):
         step = min(256, rows)
@@ -264,7 +277,7 @@
 
         lax.fori_loop(0, rows // step, go, 0)
 
-    fill(hot_own, gx * gy, cells[0] // gz)
+    fill(hot_own, gx * gy, cells[...] // gz)
 
     for copy in firsts:
         copy.wait_recv()
@@ -282,11 +295,10 @@
         seconds.append(copy)
     arrived[bx] = agg[bx]
 
-    cells_in = []
     for s in range(4):
         @pl.when(has[s])
         def _(s=s):
-            landed(cells.at[0], passed_cells.at[s], raw_recv.at[back[s]], s).wait_recv()
+            landed(cells_in.at[0], passed_cells.at[s], raw_recv.at[back[s]], s).wait_recv()
             row_id = passed_cells[s] // gz
             if s == 0:
                 fill(hot_lr.at[0], WIDE * gy, row_id - (gx - WIDE) * gy)
@@ -321,9 +333,10 @@
         def _(s=s):
             handed[s].start()
 
-    targets(lambda b: arrived[b], cells[0])
+    targets(lambda b: arrived[b], cells[...])
     loads[0].wait()
-    planes = 4
+    planes = min(4, gx)
+    ends = 2
 
     def inject_own(i, carry):
         r0 = pl.multiple_of(i * planes * gy, planes * gy)
@@ -382,14 +395,19 @@
     def v_rows(p, x, lo, hi):
         vs[x, lo:hi, :] = vs[x, lo:hi, :] - span(lambda j: p[x + WIDE, lo + j:hi + j, :])
 
-    def w_plane(p, x):
-        ws[x] = ws[x] - z_term(p[x + WIDE, PAD:PAD + gy, :], flags[x])
-
-    def p_rows(old, new, x, lo, hi):
+    def w_planes(p, new, x, shift):
+        rows = planes * gy
+        shift_y = PAD if shift else 0
+        f = p[pl.ds(x + WIDE, planes), PAD:PAD + gy, :].reshape(rows, gz)
+        flag = flags[pl.ds(x, planes)].reshape(rows, gz)
+        w = ws[pl.ds(x, planes)].reshape(rows, gz) - z_term(f, flag)
+        ws[pl.ds(x, planes)] = w.reshape(planes, gy, gz)
+        new[pl.ds(x + shift, planes), shift_y:shift_y + gy, :] = (f - z_term(w, -flag)).reshape(planes, gy, gz)
+
+    def p_rows(p, x, lo, hi):
         change = span(lambda j: us[x + REACH + j, lo:hi, :])
         change = change + span(lambda j: vs[x, PAD + lo + j:PAD + hi + j, :])
-        change = change + z_term(ws[x, lo:hi, :], -flags[x, lo:hi, :])
-        new[x + WIDE, PAD + lo:PAD + hi, :] = old[x + WIDE, PAD + lo:PAD + hi, :] - change
+        p[x + WIDE, PAD + lo:PAD + hi, :] = p[x + WIDE, PAD + lo:PAD + hi, :] - change
 
     def outer_u(p, s):
         lo = 0 if s == 0 else REACH + gx
@@ -413,9 +431,15 @@
     def first_velocity(x):
         u_plane(pa, x + REACH)
         v_rows(pa, x, PAD, PAD + gy)
-        w_plane(pa, x)
 
     loop(0, gx, first_velocity)
+    third = gx // planes - 2 * ends
+
+    def w_blocks(p, new, lo, hi, shift):
+        loop(lo, hi, lambda i: w_planes(p, new, i * planes, shift))
+
+    w_blocks(pa, pb, 0, ends, WIDE)
+    w_blocks(pa, pb, ends + third, 2 * ends + third, WIDE)
 
     give_b = (
         pb.at[pl.ds(WIDE, WIDE), y_core],
@@ -432,33 +456,24 @@
         def _():
             second_rim[s].start()
 
-    loop(0, WIDE, lambda x: p_rows(pa, pb, x, 0, gy))
+    loop(0, WIDE, lambda x: p_rows(pb, x, 0, gy))
     send_rim(0)
-    loop(gx - WIDE, gx, lambda x: p_rows(pa, pb, x, 0, gy))
+    loop(gx - WIDE, gx, lambda x: p_rows(pb, x, 0, gy))
     send_rim(1)
+    w_blocks(pa, pb, ends, ends + third, WIDE)
 
     def edges(x):
-        p_rows(pa, pb, x, 0, PAD)
-        p_rows(pa, pb, x, gy - PAD, gy)
+        p_rows(pb, x, 0, PAD)
+        p_rows(pb, x, gy - PAD, gy)
 
     loop(WIDE, gx - WIDE, edges)
     send_rim(2)
     send_rim(3)
-    loop(WIDE, gx - WIDE, lambda x: p_rows(pa, pb, x, PAD, gy - PAD))
-
-    def inner_velocity(x):
-        v_rows(pb, x, 2 * PAD, gy)
-        w_plane(pb, x)
-
-    loop(0, gx, inner_velocity)
+    loop(WIDE, gx - WIDE, lambda x: p_rows(pb, x, PAD, gy - PAD))
+
+    w_blocks(pb, pz, 0, gx // planes, 0)
+    loop(0, gx, lambda x: v_rows(pb, x, 2 * PAD, gy))
     loop(2 * REACH, gx, lambda i: u_plane(pb, i))
-    outs = [
-        pltpu.make_async_copy(pa.at[x_core, y_core], out.at[0], out_sem.at[0]),
-        pltpu.make_async_copy(us.at[pl.ds(REACH, gx)], out.at[1], out_sem.at[1]),
-        pltpu.make_async_copy(vs.at[:, y_core], out.at[2], out_sem.at[2]),
-        pltpu.make_async_copy(ws, out.at[3], out_sem.at[3]),
-    ]
-    outs[3].start()
     for s in range(4):
         @pl.when(has[s])
         def _(s=s):
@@ -467,7 +482,6 @@
         outer_u(pb, s)
     loop(REACH, 2 * REACH, lambda i: u_plane(pb, i))
     loop(gx, gx + REACH, lambda i: u_plane(pb, i))
-    outs[1].start()
     for s in (2, 3):
         outer_v(pb, s)
 
@@ -476,9 +490,6 @@
         v_rows(pb, x, gy, gy + PAD)
 
     loop(0, gx, outer_rows)
-    outs[2].start()
-    loop(0, gx, lambda x: p_rows(pb, pa, x, 0, gy))
-    outs[0].start()
 
     for copy in firsts + seconds:
         copy.wait_send()
@@ -489,7 +500,37 @@
                 copy.wait_send()
             handed[s].wait_send()
             second_rim[s].wait_send()
-    for copy in outs:
+
+
+def last_kernel(pz, us, vs, ws, out, held, sems):
+    gx, gy, gz = ws.shape
+    step = min(8, gx)
+    copies = [
+        pltpu.make_async_copy(us.at[pl.ds(REACH, gx)], out.at[1], sems.at[0]),
+        pltpu.make_async_copy(vs.at[:, pl.ds(PAD, gy)], out.at[2], sems.at[1]),
+        pltpu.make_async_copy(ws, out.at[3], sems.at[2]),
+    ]
+    for copy in copies:
+        copy.start()
+    for part in range(gx // step):
+        def plane(i, carry):
+            x = part * step + i
+            change = None
+            for j, w in enumerate(WEIGHTS, 1):
+                term = (DT * w) * (
+                    us[x + REACH + j] - us[x + REACH - j]
+                    + (vs[x, PAD + j:PAD + gy + j, :] - vs[x, PAD - j:PAD + gy - j, :])
+                )
+                change = term if change is None else change + term
+            held[x] = pz[x] - change
+            return carry
+
+        lax.fori_loop(0, step, plane, 0)
+        rows = pl.ds(part * step, step)
+        copy = pltpu.make_async_copy(held.at[rows], out.at[0, rows], sems.at[3 + part])
+        copy.start()
+        copies.append(copy)
+    for copy in copies:
         copy.wait()
 
 
@@ -508,35 +549,18 @@
     q = panel_points.shape[1]
     gx, gy, gz = fields.shape[1:]
     k = nbx * 128
-    packet = pl.pallas_call(
-        functools.partial(panel_kernel, nbx, nby),
-        out_shape=jax.ShapeDtypeStruct((devices, 128), F32),
-        in_specs=[vmem()] * 7,
-        out_specs=vmem(),
-        scratch_shapes=panel_scratch(m, q, devices),
-        compiler_params=pltpu.CompilerParams(vmem_limit_bytes=48 << 20),
-        name="panels",
-    )(
-        observers,
-        slots.reshape(1, m),
-        fractions.reshape(1, m),
-        owners.reshape(1, m),
-        panel_points,
-        panel_normals,
-        sources.transpose(0, 2, 1),
-    )
     dma = pltpu.SemaphoreType.DMA
-    return pl.pallas_call(
+    wide = (gx + 2 * WIDE, gy + 2 * PAD, gz)
+    kept = ((gx, gy, gz), (gx + 2 * REACH, gy, gz), (gx, gy + 2 * PAD, gz), (gx, gy, gz))
+    sems = (9, 4, 12, 12, nby, nby, nbx, nbx, 4, 4, 4, 4)
+    state = pl.pallas_call(
         functools.partial(box_kernel, nbx, nby),
-        out_shape=jax.ShapeDtypeStruct(fields.shape, F32),
-        in_specs=[vmem(), vmem(), vmem(), anywhere()],
-        out_specs=anywhere(),
+        out_shape=[jax.ShapeDtypeStruct(shape, F32) for shape in kept],
+        in_specs=[pl.BlockSpec(memory_space=pltpu.HBM)] * 10,
+        out_specs=[vmem()] * 4,
         scratch_shapes=[
-            pltpu.VMEM((gx + 2 * WIDE, gy + 2 * PAD, gz), F32),
-            pltpu.VMEM((gx + 2 * WIDE, gy + 2 * PAD, gz), F32),
-            pltpu.VMEM((gx + 2 * REACH, gy, gz), F32),
-            pltpu.VMEM((gx, gy + 2 * PAD, gz), F32),
-            pltpu.VMEM((gx, gy, gz), F32),
+            pltpu.VMEM(wide, F32),
+            pltpu.VMEM(wide, F32),
             pltpu.VMEM((gx, gy, gz), F32),
             pltpu.VMEM((3 * gz, 2 * gz), BF),
             pltpu.VMEM((gx * gy, k), BF),
@@ -548,24 +572,42 @@
             pltpu.VMEM((nbx, 1, 128), F32),
             pltpu.VMEM((4, nbx, 1, 128), F32),
             pltpu.VMEM((4, nbx, 128), jnp.int32),
-            dma((4,)),
-            dma((12,)),
-            dma((12,)),
-            dma((nby,)),
-            dma((nby,)),
-            dma((nbx,)),
-            dma((nbx,)),
-            dma((4,)),
-            dma((4,)),
-            dma((4,)),
-            dma((4,)),
-            dma((4,)),
-        ],
+            pltpu.VMEM((3, m), F32),
+            pltpu.VMEM((1, m), jnp.int32),
+            pltpu.VMEM((1, m), F32),
+            pltpu.VMEM((1, m), jnp.int32),
+            pltpu.VMEM((3, q), F32),
+            pltpu.VMEM((3, q), F32),
+            pltpu.VMEM((3, sources.shape[2], q), BF),
+            pltpu.VMEM((nbx, 128), jnp.int32),
+            pltpu.VMEM((gx, gy), jnp.int32),
+            pltpu.VMEM((devices, 128), F32),
+        ] + panel_scratch(m, q, devices) + [dma((n,)) for n in sems],
         compiler_params=pltpu.CompilerParams(
-            collective_id=0, has_side_effects=True, vmem_limit_bytes=56 << 20
+            collective_id=0, has_side_effects=True, vmem_limit_bytes=42 << 20
         ),
         name="box",
-    )(packet, arrival_cell, ground, fields)
+    )(
+        observers,
+        slots.reshape(1, m),
+        fractions.reshape(1, m),
+        owners.reshape(1, m),
+        panel_points,
+        panel_normals,
+        sources.transpose(0, 2, 1),
+        arrival_cell,
+        ground,
+        fields,
+    )
+    return pl.pallas_call(
+        last_kernel,
+        out_shape=jax.ShapeDtypeStruct(fields.shape, F32),
+        in_specs=[vmem()] * 4,
+        out_specs=anywhere(),
+        scratch_shapes=[pltpu.VMEM((gx, gy, gz), F32), dma((3 + gx // min(8, gx),))],
+        compiler_params=pltpu.CompilerParams(vmem_limit_bytes=8 << 20),
+        name="last",
+    )(*state)
 
 
 def solution(mesh):

time: 149 us -> 112 us (0.75)
  Pallas kernels: 133 us -> 104 us
  local copies, waits for them, and re-layouts: 14.3 us -> 7.24 us
    pallas_call x2, Pallas kernels: 133 us -> 104 us  [the longest x1 101 us: body(): pl.pallas_call(functools.partial(box_kernel, nbx, nby), out_shape=[jax.Sh...]
    unnamed x17 -> x18, local copies, waits for them, and re-layouts: 14.3 us -> 7.24 us
where the time goes in v2:
time: 112 us; the launch traced here: 111 us
  Pallas kernels  104 us (93%)
  local copies, waits for them, and re-layouts  7.24 us (6%)
    pallas_call x1, Pallas kernels, body(): pl.pallas_call(functools.partial(box_kernel, nbx, nby), out_shape=[jax.Sh...  101 us
    unnamed x18, local copies, waits for them, and re-layouts  7.24 us
    pallas_call x1, Pallas kernels, body(): pl.pallas_call(last_kernel, out_shape=jax.ShapeDtypeStruct(fields.shape,...  3.34 us

profile of v2, /device:TPU:36, one launch (start us, length us, event | category | flops | bytes accessed | tf_op | source)
XLA Modules:
  0.0 111.3 jit_solution(16746304870626501812)
XLA Ops:
  0.0 0.0 copy-start
  0.0 1.1 %copy-done = bf16[3,2048,64]{1,2,0:T(8,128)(2,1)S(1)} copy-done((bf16[3,2048,64]{1,2,0:T(8,128)(2,1)S(1)}, bf16[3,2048,64]{1,2,0:T(8,128)(2,1)}, u32[]{:S(2)}) %copy-start) | copy-done | bytes 786456
  1.1 0.0 copy-start.1
  1.1 0.9 copy-done.1
  2.0 0.0 copy-start.2
  2.0 0.8 copy-done.2
  2.8 0.0 copy-start.3
  2.8 0.8 copy-done.3
  3.6 0.0 copy-start.4
  3.6 0.8 copy-done.4
  4.3 0.0 copy-start.5
  4.3 0.8 copy-done.5
  5.1 0.0 copy-start.6
  5.1 0.8 copy-done.6
  5.8 0.0 copy-start.7
  5.8 0.7 copy-done.7
  6.5 0.0 copy-start.8
  6.6 0.7 copy-done.8
  7.2 100.7 %box.1 = (f32[32,128,128]{2,1,0:T(8,128)S(1)}, f32[38,128,128]{2,1,0:T(8,128)S(1)}, f32[32,144,128]{2,1,0:T(8,128)S(1)}, f32[32,128,128]{2,1,0:T(8,128)S(1)}) custom-call(f32[3,8192]{1,0:T(4,128)S(1)} %copy-done.1, s32[1,8192]{1,0:T(1,128)S(1)} %bitcast.5, f32[1,8192]{1,0:T(1,128)S(1)} %bitcast.6, s32[1,8192]{1,0:T(1,128)S(1)} %bitcast.7, ...), custom_call_target="tpu_custom_call" | custom-call | tf_op jit(solution)/shard_map/box/pallas_call | solution.py:556
  108.0 3.3 %last.1 = f32[4,32,128,128]{3,2,1,0:T(8,128)} custom-call(f32[32,128,128]{2,1,0:T(8,128)S(1)} %get-tuple-element.9.pz, f32[38,128,128]{2,1,0:T(8,128)S(1)} %get-tuple-element.10.us, f32[32,144,128]{2,1,0:T(8,128)S(1)} %get-tuple-element.11.vs, f32[32,128,128]{2,1,0:T(8,128)S(1)} %get-tuple-element.12.ws), custom_call_target="tpu_custom_call" | custom-call | tf_op jit(solution)/shard_map/last/pallas_call | solution.py:602
Async XLA Ops:
  0.0 1.1 %copy-start = (bf16[3,2048,64]{1,2,0:T(8,128)(2,1)S(1)}, bf16[3,2048,64]{1,2,0:T(8,128)(2,1)}, u32[]{:S(2)}) copy-start(bf16[3,2048,64]{1,2,0:T(8,128)(2,1)} %param.19) | copy-start | bytes 2359300
  1.1 0.9 copy-start.1
  2.0 0.8 copy-start.2
  2.8 0.8 copy-start.3
  3.6 0.8 copy-start.4
  4.3 0.8 copy-start.5
  5.1 0.8 copy-start.6
  5.8 0.7 copy-start.7
  6.5 0.7 copy-start.8

commit v3 on v2

--- a/solution.py
+++ b/solution.py
@@ -163,7 +163,6 @@
         pl.semaphore_signal(barrier, inc=1, device_id=(bx, lax.rem(by + i, nby)), device_id_type=MESH)
     for i in range(1, nbx):
         pl.semaphore_signal(barrier, inc=1, device_id=(lax.rem(bx + i, nbx), by), device_id_type=MESH)
-    pl.semaphore_wait(barrier, nby - 1 + nbx - 1)
 
     def remote(src, dst, send, recv, target):
         return pltpu.make_async_remote_copy(
@@ -213,12 +212,6 @@
     def landed(src, dst, recv, s):
         return remote(src, dst, raw_send.at[s], recv, to[s % 4])
 
-    for s in range(4):
-        @pl.when(has[s])
-        def _(s=s):
-            for copy in raw[s]:
-                copy.start()
-
     loads = [
         pltpu.make_async_copy(fields.at[0], pa.at[x_core, y_core], load_sem.at[0]),
         pltpu.make_async_copy(fields.at[1], us.at[pl.ds(REACH, gx)], load_sem.at[1]),
@@ -253,6 +246,13 @@
     ground_t = ground[...].astype(F32).T
     for x in range(gx):
         flags[x] = jnp.broadcast_to(ground_t[:, x:x + 1], (gy, gz))
+
+    pl.semaphore_wait(barrier, nby - 1 + nbx - 1)
+    for s in range(4):
+        @pl.when(has[s])
+        def _(s=s):
+            for copy in raw[s]:
+                copy.start()
 
     panel_part(nbx, nby, obs, slots, fracs, owners, pts, nrm, src, packet, eo, ep, feat, pieces, base)
     firsts = []
@@ -311,7 +311,7 @@
 
     heights = lax.broadcasted_iota(jnp.int32, (gz, 1), 0)
 
-    def targets(values, cell_rows):
+    def targets(bt, values, cell_rows):
         for b in range(nbx):
             v = values(b)
             at = heights == cell_rows[b:b + 1, :] % gz
@@ -319,7 +319,7 @@
             bt[0:gz, b * 128:(b + 1) * 128] = jnp.where(at, hi, 0.0).astype(BF)
             bt[gz:2 * gz, b * 128:(b + 1) * 128] = jnp.where(at, v - hi, 0.0).astype(BF)
 
-    def added(hot):
+    def added(hot, bt):
         both = dot_nt(hot, bt[...])
         return both[:, :gz] + both[:, gz:]
 
@@ -333,18 +333,27 @@
         def _(s=s):
             handed[s].start()
 
-    targets(lambda b: arrived[b], cells[...])
+    own, theirs = bt.at[0], bt.at[1]
+    targets(own, lambda b: arrived[b], cells[...])
     loads[0].wait()
     planes = min(4, gx)
     ends = 2
-
-    def inject_own(i, carry):
-        r0 = pl.multiple_of(i * planes * gy, planes * gy)
-        extra = added(hot_own[pl.ds(r0, planes * gy), :]).reshape(planes, gy, gz)
-        pa[pl.ds(WIDE + i * planes, planes), PAD:PAD + gy, :] += extra
-        return carry
-
-    lax.fori_loop(0, gx // planes, inject_own, 0)
+    near = min(2 * WIDE, gx // 2)
+
+    def inject_own(lo, hi):
+        count = hi - lo
+        step = next(n for n in (6, 4, 2, 1) if count % n == 0)
+
+        def go(i, carry):
+            x = lo + i * step
+            rows = pl.ds(pl.multiple_of(x * gy, gy), step * gy)
+            pa[pl.ds(WIDE + x, step), PAD:PAD + gy, :] += added(hot_own[rows, :], own).reshape(step, gy, gz)
+            return carry
+
+        lax.fori_loop(0, count // step, go, 0)
+
+    inject_own(0, near)
+    inject_own(gx - near, gx)
 
     for s in range(4):
         @pl.when(has[s])
@@ -352,19 +361,13 @@
             landed(give_p[s], rim_a[s], raw_recv.at[4 + back[s]], 4 + s).wait_recv()
             landed(give_v[s], rim_v[s], raw_recv.at[8 + back[s]], 8 + s).wait_recv()
             remote(arrived, passed.at[s], nb_send.at[s], nb_recv.at[back[s]], to[s]).wait_recv()
-            targets(lambda b: passed[s, b], passed_cells[s])
+            targets(theirs, lambda b: passed[s, b], passed_cells[s])
             if s < 2:
                 x0 = 0 if s == 0 else WIDE + gx
-
-                def inject_x(i, carry):
-                    r0 = pl.multiple_of(i * gy, gy)
-                    pa[x0 + i, PAD:PAD + gy, :] += added(hot_lr[s, pl.ds(r0, gy), :])
-                    return carry
-
-                lax.fori_loop(0, WIDE, inject_x, 0)
+                pa[x0:x0 + WIDE, PAD:PAD + gy, :] += added(hot_lr[s], theirs).reshape(WIDE, gy, gz)
             else:
                 y0 = 0 if s == 2 else PAD + gy
-                pa[WIDE:WIDE + gx, y0:y0 + PAD, :] += added(hot_du[s - 2]).reshape(gx, PAD, gz)
+                pa[WIDE:WIDE + gx, y0:y0 + PAD, :] += added(hot_du[s - 2], theirs).reshape(gx, PAD, gz)
 
     for copy in loads[1:]:
         copy.wait()
@@ -416,23 +419,24 @@
         def _():
             loop(lo, lo + REACH, lambda i: u_plane(p, i))
 
-    def outer_v(p, s):
+    def outer_v(p, s, x0, x1):
         lo = PAD - REACH if s == 2 else PAD + gy
 
         @pl.when(has[s])
         def _():
-            loop(0, gx, lambda x: v_rows(p, x, lo, lo + REACH))
+            loop(x0, x1, lambda x: v_rows(p, x, lo, lo + REACH))
 
     for s in (0, 1):
         outer_u(pa, s)
     for s in (2, 3):
-        outer_v(pa, s)
-
-    def first_velocity(x):
-        u_plane(pa, x + REACH)
-        v_rows(pa, x, PAD, PAD + gy)
-
-    loop(0, gx, first_velocity)
+        outer_v(pa, s, 0, WIDE)
+        outer_v(pa, s, gx - WIDE, gx)
+
+    few = min(WIDE + REACH, gx // 2)
+    loop(REACH, REACH + few, lambda i: u_plane(pa, i))
+    loop(REACH + gx - few, REACH + gx, lambda i: u_plane(pa, i))
+    loop(0, WIDE, lambda x: v_rows(pa, x, PAD, PAD + gy))
+    loop(gx - WIDE, gx, lambda x: v_rows(pa, x, PAD, PAD + gy))
     third = gx // planes - 2 * ends
 
     def w_blocks(p, new, lo, hi, shift):
@@ -460,7 +464,13 @@
     send_rim(0)
     loop(gx - WIDE, gx, lambda x: p_rows(pb, x, 0, gy))
     send_rim(1)
+    if gx > 2 * near:
+        inject_own(near, gx - near)
+    for s in (2, 3):
+        outer_v(pa, s, WIDE, gx - WIDE)
+    loop(WIDE, gx - WIDE, lambda x: v_rows(pa, x, PAD, PAD + gy))
     w_blocks(pa, pb, ends, ends + third, WIDE)
+    loop(REACH + few, REACH + gx - few, lambda i: u_plane(pa, i))
 
     def edges(x):
         p_rows(pb, x, 0, PAD)
@@ -483,7 +493,7 @@
     loop(REACH, 2 * REACH, lambda i: u_plane(pb, i))
     loop(gx, gx + REACH, lambda i: u_plane(pb, i))
     for s in (2, 3):
-        outer_v(pb, s)
+        outer_v(pb, s, 0, gx)
 
     def outer_rows(x):
         v_rows(pb, x, PAD, 2 * PAD)
@@ -566,7 +576,7 @@
             pltpu.VMEM((gx * gy, k), BF),
             pltpu.VMEM((2, WIDE * gy, k), BF),
             pltpu.VMEM((2, gx * PAD, k), BF),
-            pltpu.VMEM((2 * gz, k), BF),
+            pltpu.VMEM((2, 2 * gz, k), BF),
             pltpu.VMEM((nby, nbx, 128), F32),
             pltpu.VMEM((nbx, 1, 128), F32),
             pltpu.VMEM((nbx, 1, 128), F32),
@@ -584,10 +594,10 @@
             pltpu.VMEM((devices, 128), F32),
         ] + panel_scratch(m, q, devices) + [dma((n,)) for n in sems],
         compiler_params=pltpu.CompilerParams(
-            collective_id=0, has_side_effects=True, vmem_limit_bytes=42 << 20
+            collective_id=0, has_side_effects=True, vmem_limit_bytes=44 << 20
         ),
         name="box",
-    )(
+    )(*[pltpu.with_memory_space_constraint(v, pltpu.HBM) for v in (
         observers,
         slots.reshape(1, m),
         fractions.reshape(1, m),
@@ -598,7 +608,7 @@
         arrival_cell,
         ground,
         fields,
-    )
+    )])
     return pl.pallas_call(
         last_kernel,
         out_shape=jax.ShapeDtypeStruct(fields.shape, F32),

time: 112 us -> 95.6 us (0.85)
  Pallas kernels: 104 us -> 95.5 us
  local copies, waits for them, and re-layouts: 7.24 us -> 0 us
    pallas_call x1, Pallas kernels: 101 us -> 92.2 us  [body(): pl.pallas_call(functools.partial(box_kernel, nbx, nby), out_shape=[jax.Sh...]
    unnamed x18 -> x0, local copies, waits for them, and re-layouts: 7.24 us -> none
where the time goes in v3:
time: 95.6 us; the launch traced here: 95.5 us
  Pallas kernels  95.5 us (100%)
    pallas_call x1, Pallas kernels, body(): pl.pallas_call(functools.partial(box_kernel, nbx, nby), out_shape=[jax.Sh...  92.2 us
    pallas_call x1, Pallas kernels, body(): pl.pallas_call(last_kernel, out_shape=jax.ShapeDtypeStruct(fields.shape,...  3.34 us

profile of v3, /device:TPU:36, one launch (start us, length us, event | category | flops | bytes accessed | tf_op | source)
XLA Modules:
  0.0 95.5 jit_solution(183313053897877516)
XLA Ops:
  0.0 92.2 %box.1 = (f32[32,128,128]{2,1,0:T(8,128)S(1)}, f32[38,128,128]{2,1,0:T(8,128)S(1)}, f32[32,144,128]{2,1,0:T(8,128)S(1)}, f32[32,128,128]{2,1,0:T(8,128)S(1)}) custom-call(f32[3,8192]{1,0:T(4,128)} %obs_in.1, s32[1,8192]{1,0:T(1,128)} %bitcast.5, f32[1,8192]{1,0:T(1,128)} %bitcast.6, s32[1,8192]{1,0:T(1,128)} %bitcast.7, f32[3,2048]{1,0:T(4,128)} %pts_in.1, ...), custom_call_target="tpu_custom_call" | custom-call | tf_op jit(solution)/shard_map/box/pallas_call | solution.py:566
  92.2 3.3 %last.1 = f32[4,32,128,128]{3,2,1,0:T(8,128)} custom-call(f32[32,128,128]{2,1,0:T(8,128)S(1)} %get-tuple-element.9.pz, f32[38,128,128]{2,1,0:T(8,128)S(1)} %get-tuple-element.10.us, f32[32,144,128]{2,1,0:T(8,128)S(1)} %get-tuple-element.11.vs, f32[32,128,128]{2,1,0:T(8,128)S(1)} %get-tuple-element.12.ws), custom_call_target="tpu_custom_call" | custom-call | tf_op jit(solution)/shard_map/last/pallas_call | solution.py:612

commit v4 on v3

--- a/solution.py
+++ b/solution.py
@@ -44,14 +44,15 @@
     ]
 
 
-def panel_part(nbx, nby, obs, slots, fracs, owners, pts, nrm, src, packet, eo, ep, feat, pieces, base):
+def panel_part(nbx, nby, obs, slots, fracs, owners, pts, nrm, src, packet, eo, ep, feat, pieces, base, kern, ready):
     m = obs.shape[1]
     q = pts.shape[1]
     samples = src.shape[1]
     devices = nbx * nby
-    tile = min(1024, m)
+    tile = min(1024, m, kern.shape[1])
     chunk = min(512, q)
     sub = 256
+    block = 256
 
     o = obs[...]
     eo[0:3, :] = o
@@ -76,6 +77,7 @@
     ep[3:4, :] = jnp.zeros((1, q), F32)
     ep[4:5, :] = -jnp.sum(p * n, axis=0, keepdims=True)
     lay(1)
+    ready()
     pieces[...] = jnp.zeros_like(pieces)
     base[...] = jnp.zeros_like(base)
     row = lax.broadcasted_iota(jnp.int32, (devices, 1), 0)
@@ -97,12 +99,18 @@
         def one_chunk(c, acc):
             q0 = pl.multiple_of(c * chunk, chunk)
             rows = pl.ds(q0, chunk)
-            inverse = lax.rsqrt(dot(feat[0, rows, :], of))
-            near = dot(feat[1, rows, :], of) * inverse * inverse
-            far = near * inverse
-            acc = acc + dot(src[0, :, rows], inverse.astype(BF))
-            acc = acc + dot(src[1, :, rows], near.astype(BF))
-            return acc + dot(src[2, :, rows], far.astype(BF))
+            for l in range(0, tile, block):
+                wide = slice(l, l + block)
+                for r in range(0, chunk, block):
+                    some = pl.ds(q0 + r, block)
+                    inverse = lax.rsqrt(dot(feat[0, some, :], of[:, wide]))
+                    near = dot(feat[1, some, :], of[:, wide]) * inverse * inverse
+                    kern[r:r + block, wide] = inverse.astype(BF)
+                    kern[chunk + r:chunk + r + block, wide] = near.astype(BF)
+                    kern[2 * chunk + r:2 * chunk + r + block, wide] = (near * inverse).astype(BF)
+            for k in range(3):
+                acc = acc + dot(src[k, :, rows], kern[k * chunk:(k + 1) * chunk, 0:tile])
+            return acc
 
         history = lax.fori_loop(0, q // chunk, one_chunk, jnp.zeros((samples, tile), F32))
         slot = slots[:, here]
@@ -247,14 +255,17 @@
     for x in range(gx):
         flags[x] = jnp.broadcast_to(ground_t[:, x:x + 1], (gy, gz))
 
-    pl.semaphore_wait(barrier, nby - 1 + nbx - 1)
-    for s in range(4):
-        @pl.when(has[s])
-        def _(s=s):
-            for copy in raw[s]:
-                copy.start()
-
-    panel_part(nbx, nby, obs, slots, fracs, owners, pts, nrm, src, packet, eo, ep, feat, pieces, base)
+    def greet_and_send():
+        pl.semaphore_wait(barrier, nby - 1 + nbx - 1)
+        for s in range(4):
+            @pl.when(has[s])
+            def _(s=s):
+                for copy in raw[s]:
+                    copy.start()
+
+
+    panel_part(nbx, nby, obs, slots, fracs, owners, pts, nrm, src, packet, eo, ep, feat, pieces, base,
+               hot_own, greet_and_send)
     firsts = []
     for i in range(1, nby):
         peer = lax.rem(by + i, nby)

time: 95.6 us -> 91.9 us (0.961)
  Pallas kernels: 95.5 us -> 91.8 us
    pallas_call x1, Pallas kernels: 92.2 us -> 88.5 us  [body(): pl.pallas_call(functools.partial(box_kernel, nbx, nby), out_shape=[jax.Sh...]
where the time goes in v4:
time: 91.9 us; the launch traced here: 91.8 us
  Pallas kernels  91.8 us (100%)
    pallas_call x1, Pallas kernels, body(): pl.pallas_call(functools.partial(box_kernel, nbx, nby), out_shape=[jax.Sh...  88.5 us
    pallas_call x1, Pallas kernels, body(): pl.pallas_call(last_kernel, out_shape=jax.ShapeDtypeStruct(fields.shape,...  3.34 us

profile of v4, /device:TPU:36, one launch (start us, length us, event | category | flops | bytes accessed | tf_op | source)
XLA Modules:
  0.0 91.8 jit_solution(648849988480854897)
XLA Ops:
  0.0 88.5 %box.1 = (f32[32,128,128]{2,1,0:T(8,128)S(1)}, f32[38,128,128]{2,1,0:T(8,128)S(1)}, f32[32,144,128]{2,1,0:T(8,128)S(1)}, f32[32,128,128]{2,1,0:T(8,128)S(1)}) custom-call(f32[3,8192]{1,0:T(4,128)} %obs_in.1, s32[1,8192]{1,0:T(1,128)} %bitcast.5, f32[1,8192]{1,0:T(1,128)} %bitcast.6, s32[1,8192]{1,0:T(1,128)} %bitcast.7, f32[3,2048]{1,0:T(4,128)} %pts_in.1, ...), custom_call_target="tpu_custom_call" | custom-call | tf_op jit(solution)/shard_map/box/pallas_call | solution.py:577
  88.5 3.3 %last.1 = f32[4,32,128,128]{3,2,1,0:T(8,128)} custom-call(f32[32,128,128]{2,1,0:T(8,128)S(1)} %get-tuple-element.9.pz, f32[38,128,128]{2,1,0:T(8,128)S(1)} %get-tuple-element.10.us, f32[32,144,128]{2,1,0:T(8,128)S(1)} %get-tuple-element.11.vs, f32[32,128,128]{2,1,0:T(8,128)S(1)} %get-tuple-element.12.ws), custom_call_target="tpu_custom_call" | custom-call | tf_op jit(solution)/shard_map/last/pallas_call | solution.py:623

commit v5 on v4

--- a/solution.py
+++ b/solution.py
@@ -401,7 +401,7 @@
             step(i)
             return carry
 
-        lax.fori_loop(lo, hi, go, 0)
+        lax.fori_loop(lo, hi, go, 0, unroll=2 if (hi - lo) % 2 == 0 else 1)
 
     def u_plane(p, i):
         us[i] = us[i] - span(lambda j: p[i + REACH + j, PAD:PAD + gy, :])

time: 91.9 us -> 90.1 us (0.980)
  Pallas kernels: 91.8 us -> 90 us
    pallas_call x1, Pallas kernels: 88.5 us -> 86.7 us  [body(): pl.pallas_call(functools.partial(box_kernel, nbx, nby), out_shape=[jax.Sh...]
where the time goes in v5:
time: 90.1 us; the launch traced here: 90 us
  Pallas kernels  90 us (100%)
    pallas_call x1, Pallas kernels, body(): pl.pallas_call(functools.partial(box_kernel, nbx, nby), out_shape=[jax.Sh...  86.7 us
    pallas_call x1, Pallas kernels, body(): pl.pallas_call(last_kernel, out_shape=jax.ShapeDtypeStruct(fields.shape,...  3.34 us

profile of v5, /device:TPU:36, one launch (start us, length us, event | category | flops | bytes accessed | tf_op | source)
XLA Modules:
  0.0 90.0 jit_solution(4705193440592498281)
XLA Ops:
  0.0 86.7 %box.1 = (f32[32,128,128]{2,1,0:T(8,128)S(1)}, f32[38,128,128]{2,1,0:T(8,128)S(1)}, f32[32,144,128]{2,1,0:T(8,128)S(1)}, f32[32,128,128]{2,1,0:T(8,128)S(1)}) custom-call(f32[3,8192]{1,0:T(4,128)} %obs_in.1, s32[1,8192]{1,0:T(1,128)} %bitcast.5, f32[1,8192]{1,0:T(1,128)} %bitcast.6, s32[1,8192]{1,0:T(1,128)} %bitcast.7, f32[3,2048]{1,0:T(4,128)} %pts_in.1, ...), custom_call_target="tpu_custom_call" | custom-call | tf_op jit(solution)/shard_map/box/pallas_call | solution.py:577
  86.7 3.3 %last.1 = f32[4,32,128,128]{3,2,1,0:T(8,128)} custom-call(f32[32,128,128]{2,1,0:T(8,128)S(1)} %get-tuple-element.9.pz, f32[38,128,128]{2,1,0:T(8,128)S(1)} %get-tuple-element.10.us, f32[32,144,128]{2,1,0:T(8,128)S(1)} %get-tuple-element.11.vs, f32[32,128,128]{2,1,0:T(8,128)S(1)} %get-tuple-element.12.ws), custom_call_target="tpu_custom_call" | custom-call | tf_op jit(solution)/shard_map/last/pallas_call | solution.py:623

commit v6 on v5

--- a/solution.py
+++ b/solution.py
@@ -401,7 +401,7 @@
             step(i)
             return carry
 
-        lax.fori_loop(lo, hi, go, 0, unroll=2 if (hi - lo) % 2 == 0 else 1)
+        lax.fori_loop(lo, hi, go, 0, unroll=next(n for n in (2, 3, 1) if (hi - lo) % n == 0))
 
     def u_plane(p, i):
         us[i] = us[i] - span(lambda j: p[i + REACH + j, PAD:PAD + gy, :])

time: 90.1 us -> 90.1 us (level)
  no operation moved by 1% of the time
where the time goes in v6:
time: 90.1 us; the launch traced here: 90 us
  Pallas kernels  89.8 us (100%)
    pallas_call x1, Pallas kernels, body(): pl.pallas_call(functools.partial(box_kernel, nbx, nby), out_shape=[jax.Sh...  86.5 us
    pallas_call x1, Pallas kernels, body(): pl.pallas_call(last_kernel, out_shape=jax.ShapeDtypeStruct(fields.shape,...  3.34 us

profile of v6, /device:TPU:36, one launch (start us, length us, event | category | flops | bytes accessed | tf_op | source)
XLA Modules:
  0.0 90.0 jit_solution(16974868434178722343)
XLA Ops:
  0.0 86.5 %box.1 = (f32[32,128,128]{2,1,0:T(8,128)S(1)}, f32[38,128,128]{2,1,0:T(8,128)S(1)}, f32[32,144,128]{2,1,0:T(8,128)S(1)}, f32[32,128,128]{2,1,0:T(8,128)S(1)}) custom-call(f32[3,8192]{1,0:T(4,128)} %obs_in.1, s32[1,8192]{1,0:T(1,128)} %bitcast.5, f32[1,8192]{1,0:T(1,128)} %bitcast.6, s32[1,8192]{1,0:T(1,128)} %bitcast.7, f32[3,2048]{1,0:T(4,128)} %pts_in.1, ...), custom_call_target="tpu_custom_call" | custom-call | tf_op jit(solution)/shard_map/box/pallas_call | solution.py:577
  86.5 3.3 %last.1 = f32[4,32,128,128]{3,2,1,0:T(8,128)} custom-call(f32[32,128,128]{2,1,0:T(8,128)S(1)} %get-tuple-element.9.pz, f32[38,128,128]{2,1,0:T(8,128)S(1)} %get-tuple-element.10.us, f32[32,144,128]{2,1,0:T(8,128)S(1)} %get-tuple-element.11.vs, f32[32,128,128]{2,1,0:T(8,128)S(1)} %get-tuple-element.12.ws), custom_call_target="tpu_custom_call" | custom-call | tf_op jit(solution)/shard_map/last/pallas_call | solution.py:623
